TPU v7x, 32 devices: a whole 2x2x4 slice. The times are simulated.
32 devices in a mesh: dp: 8 (over y, x, core), fsdp: 4 (over z).
Axes of the slice: x: 2, y: 2, z: 4, core: 2. Of those that a mesh axis runs over, the one named last changes fastest.
Arguments:
- waveform: bfloat16 [1024, 50], P(('dp', 'fsdp')), may hold values from -6 to 6
- destination: int32 [1024, 1], P(('dp', 'fsdp')), may hold values from 0 to 7; in each aligned block of 32 rows (0 to 31, 32 to 63, ...) at most 8 rows name the same one
- lengths: int32 [1024], P(('dp', 'fsdp')), may hold values from 20 to 50
- conv0_weight: bfloat16 [10, 512], replicated, may hold values from -2 to 2
- conv1_weight: bfloat16 [1536, 512], replicated, may hold values from -0.15625 to 0.15625
- norm_gain: float32 [3, 512], replicated, may hold values from 0.1 to 1.9
- norm_bias: float32 [3, 512], replicated, may hold values from -3 to 3
- proj_weight: bfloat16 [512, 1920], P(None, 'fsdp'), may hold values from -0.25 to 0.25
- proj_bias: bfloat16 [1920], P('fsdp'), may hold values from -3 to 3
- cotangent: bfloat16 [2048, 4, 1920], P(('dp', 'fsdp')), may hold values from -0.1875 to 0.1875
Outputs:
- features: bfloat16 [2048, 4, 1920], P(('dp', 'fsdp'))
- grad_proj_weight: bfloat16 [512, 1920], P(None, 'fsdp')
- grad_proj_bias: bfloat16 [1920], P('fsdp')
Inputs may be any that keep to these rules, and one draw needn't show every extreme that they name: On each device no destination is named by more than 8 of its rows, and on some devices one destination is named by exactly 8 rows.
All inputs are finite; a program needn't handle non-finite values.
Results may differ from a plain program's by a relative error of at most 0.0064.
Values may be sent and summed in bfloat16 or wider, within the bound.
A program may use at most 64 MiB of HBM per device.

v0:
```python
import jax
import jax.numpy as jnp
from jax import lax
from jax.sharding import PartitionSpec as P


def layer_norm(values, gain_vec, bias_vec):
    avg_value = jnp.mean(values, axis=-1, keepdims=True)
    centred = values - avg_value
    variance = jnp.mean(centred * centred, axis=-1, keepdims=True)
    return centred * lax.rsqrt(variance + 1e-05) * gain_vec + bias_vec


def encode(wave_rows, conv0_weight, conv1_weight, norm_gain, norm_bias):
    row_count = wave_rows.shape[0]
    frame_count = (wave_rows.shape[1] - 10) // 10
    sample_blocks = wave_rows.reshape(row_count, 2 * frame_count + 2, 5)
    sample_pairs = jnp.concatenate([sample_blocks[:, :-1], sample_blocks[:, 1:]], axis=2).reshape(
        -1, 10
    )
    first_conv = jnp.dot(sample_pairs, conv0_weight, preferred_element_type=jnp.float32)
    first_conv = jax.nn.gelu(
        layer_norm(first_conv, norm_gain[0], norm_bias[0]), approximate=False
    ).astype(jnp.bfloat16)
    first_conv = first_conv.reshape(row_count, 2 * frame_count + 1, -1)
    conv_taps = jnp.concatenate(
        [
            first_conv[:, 0 : 2 * frame_count : 2],
            first_conv[:, 1 : 2 * frame_count + 1 : 2],
            first_conv[:, 2 : 2 * frame_count + 2 : 2],
        ],
        axis=2,
    )
    second_conv = jnp.dot(
        conv_taps.reshape(row_count * frame_count, -1),
        conv1_weight,
        preferred_element_type=jnp.float32,
    )
    return jax.nn.gelu(
        layer_norm(second_conv, norm_gain[1], norm_bias[1]), approximate=False
    ).astype(jnp.bfloat16)


def local(
    waveform,
    destination,
    lengths,
    conv0_weight,
    conv1_weight,
    norm_gain,
    norm_bias,
    proj_weight,
    proj_bias,
    cotangent,
):
    dp_size = lax.axis_size("dp")
    row_count = waveform.shape[0]
    slot_count = cotangent.shape[0]
    frame_count = cotangent.shape[1]
    slot_cap = slot_count // dp_size
    weights, biases = (
        lax.all_gather(proj_weight, "fsdp", axis=1, tiled=True),
        lax.all_gather(proj_bias, "fsdp", axis=0, tiled=True),
    )
    targets = destination[:, 0]
    row_order = jnp.arange(row_count, dtype=jnp.int32)
    same_dest = targets[:, None] == targets[None, :]
    earlier_rows = row_order[None, :] < row_order[:, None]
    row_rank = jnp.sum((same_dest & earlier_rows).astype(jnp.int32), axis=1)
    position = targets * slot_cap + row_rank
    placing = position[None, :] == jnp.arange(slot_count, dtype=jnp.int32)[:, None]
    slot_length = jnp.sum(jnp.where(placing, lengths[None, :], 0), axis=1)
    placing_matrix = placing.astype(jnp.bfloat16)
    slot_wave = jnp.dot(placing_matrix, waveform, preferred_element_type=jnp.float32).astype(
        jnp.bfloat16
    )
    got_wave, got_length = (
        lax.all_to_all(
            slot_wave.reshape(dp_size, slot_cap, -1), "dp", split_axis=0, concat_axis=0, tiled=True
        ),
        lax.all_to_all(
            slot_length.reshape(dp_size, slot_cap), "dp", split_axis=0, concat_axis=0, tiled=True
        ),
    )
    hidden = encode(
        got_wave.reshape(slot_count, -1), conv0_weight, conv1_weight, norm_gain, norm_bias
    )
    got_length = got_length.reshape(slot_count)
    normed = layer_norm(hidden.astype(jnp.float32), norm_gain[2], norm_bias[2]).astype(jnp.bfloat16)
    frame_ids = jnp.arange(frame_count, dtype=jnp.int32)
    valid = (10 * frame_ids[None, :] + 20 <= got_length[:, None]).reshape(-1, 1)
    frame_mask = valid.astype(jnp.float32)
    projected = jnp.dot(normed, weights, preferred_element_type=jnp.float32) + biases.astype(
        jnp.float32
    )
    features = (projected * frame_mask).astype(jnp.bfloat16).reshape(slot_count, frame_count, -1)
    cot_rows = cotangent.reshape(slot_count * frame_count, -1)
    grad_out = jnp.where(valid, cot_rows, jnp.zeros_like(cot_rows))
    weight_term = lax.dot_general(
        normed, grad_out, (((0,), (0,)), ((), ())), preferred_element_type=jnp.float32
    )
    bias_term = jnp.sum(grad_out, axis=0, dtype=jnp.float32)
    part_weight, part_bias = (
        lax.psum_scatter(weight_term, "fsdp", scatter_dimension=1, tiled=True),
        lax.psum_scatter(bias_term, "fsdp", scatter_dimension=0, tiled=True),
    )
    grad_weight, grad_bias = lax.psum((part_weight, part_bias), "dp")
    return (features, grad_weight.astype(jnp.bfloat16), grad_bias.astype(jnp.bfloat16))


def solution(mesh):
    in_specs = (
        P(("dp", "fsdp"), None),
        P(("dp", "fsdp"), None),
        P(("dp", "fsdp")),
        P(),
        P(),
        P(),
        P(),
        P(None, "fsdp"),
        P("fsdp"),
        P(("dp", "fsdp"), None, None),
    )
    out_specs = (P(("dp", "fsdp"), None, None), P(None, "fsdp"), P("fsdp"))
    return jax.shard_map(local, mesh=mesh, in_specs=in_specs, out_specs=out_specs, check_vma=False)
```

profile of v0, /device:TPU:1, one launch (start us, length us, event | category | flops | bytes accessed | tf_op | source)
XLA Modules:
  0.0 177.6 jit_solution(14233525286497537518)
XLA Ops:
  7.2 0.0 copy-start
  7.2 1.0 convert_reduce_fusion.2
  8.1 0.7 multiply_add_fusion.3
  8.8 0.7 select_reduce_fusion
  9.6 0.7 all_to_all.10
  10.2 5.2 %all-to-all-start.1 = ((s32[8,1,8]{2,1,0:T(1,128)}), s32[8,1,8]{2,1,0:T(1,128)S(1)}, u32[]{:S(2)}, u32[]{:S(2)}) async-start(s32[8,1,8]{2,1,0:T(1,128)} %bitcast.9), calls=%async_computation.1 | async-start | bytes 8192 | tf_op jit(solution)/shard_map/all_to_all | solution.py:81
  15.5 0.0 all-gather.2.cloned.1.call-start
  15.5 0.7 all-gather.2.cloned.1.call-update
  16.2 0.9 convolution_convert_fusion
  17.1 0.1 copy.20
  17.2 0.8 fusion.39
  18.0 0.8 fusion.40
  18.8 0.7 reshape.136
  19.5 0.0 copy-start.2
  19.5 1.7 reshape.120
  21.2 0.0 all-to-all-done.1
  21.3 4.2 %all-to-all-start = ((bf16[8,2,200]{2,1,0:T(2,128)(2,1)}), bf16[8,2,200]{2,1,0:T(2,128)(2,1)S(1)}, u32[]{:S(2)}, u32[]{:S(2)}) async-start(bf16[8,2,200]{2,1,0:T(2,128)(2,1)} %reshape.136), calls=%async_computation | async-start | bytes 16384 | tf_op jit(solution)/shard_map/all_to_all | solution.py:78
  25.5 0.0 reduce-scatter.2.cloned.1.call-start
  25.5 0.5 broadcast.120
  26.0 0.7 reduce.4
  26.6 0.1 le.28
  26.7 0.1 broadcast_compare_fusion
  26.8 0.1 le.31
  26.9 2.5 %all-to-all-done = bf16[8,2,200]{2,1,0:T(2,128)(2,1)S(1)} async-done(((bf16[8,2,200]{2,1,0:T(2,128)(2,1)}), bf16[8,2,200]{2,1,0:T(2,128)(2,1)S(1)}, u32[]{:S(2)}, u32[]{:S(2)}) %all-to-all-start) | async-done | bytes 6432 | tf_op jit(solution)/shard_map/all_to_all | solution.py:78
  29.5 0.1 reshape.137
  29.6 0.2 copy.21
  29.7 0.1 reshape_reshape.3
  29.9 0.2 copy.22
  30.1 0.2 reshape.116
  30.3 0.0 copy-done.2
  30.3 0.4 fusion.42
  30.8 0.3 multiply_reduce_fusion
  31.1 3.3 %fusion.4 = bf16[576,512]{1,0:T(8,128)(2,1)S(1)} fusion(f32[576,512]{1,0:T(8,128)S(1)} %get-tuple-element.18, f32[512]{0:T(512)S(1)} %bitcast.30, f32[512]{0:T(512)S(1)} %bitcast.29, f32[576]{0:T(1024)S(1)} %add_rsqrt_fusion, f32[576]{0:T(1024)S(1)} %broadcast_multiply_fusion), kind=kLoop, calls=%fused_computation.7 | loop fusion | flops 20348928 | bytes 1778176 | tf_op jit(solution)/shard_map/convert_element_type | solution.py:24
  34.4 1.2 reshape.117
  35.6 6.0 %slice.37 = bf16[64,4,512]{2,1,0:T(4,128)(2,1)} slice(bf16[64,9,512]{2,1,0:T(8,128)(2,1)} %reshape.117), slice={[0:64:1], [0:8:2], [0:512:1]} | slice | bytes 524288 | tf_op jit(solution)/shard_map/slice | solution.py:28
  41.6 6.0 %slice.38 = bf16[64,4,512]{2,1,0:T(4,128)(2,1)} slice(bf16[64,9,512]{2,1,0:T(8,128)(2,1)} %reshape.117), slice={[0:64:1], [1:9:2], [0:512:1]} | slice | bytes 524288 | tf_op jit(solution)/shard_map/slice | solution.py:29
  47.6 6.1 %slice.39 = bf16[64,4,512]{2,1,0:T(4,128)(2,1)} slice(bf16[64,9,512]{2,1,0:T(8,128)(2,1)} %reshape.117), slice={[0:64:1], [2:9:2], [0:512:1]} | slice | bytes 524288 | tf_op jit(solution)/shard_map/slice | solution.py:30
  53.6 1.5 pad_maximum_fusion
  55.1 1.1 reshape.118
  56.1 0.0 copy-done
  56.1 1.8 %fusion.43 = (f32[256]{0:T(256)S(1)}, f32[256,512]{1,0:T(8,128)S(1)}) fusion(bf16[256,1536]{1,0:T(8,128)(2,1)} %reshape.118, bf16[1536,512]{1,0:T(8,128)(2,1)S(1)} %copy-done), kind=kOutput, calls=%fused_computation.82 | convolution fusion | flops 402784000 | bytes 2884608 | tf_op jit(solution)/shard_map/dot_general | solution.py:34
  57.9 0.2 multiply_reduce_fusion.1
  58.2 1.4 convert_reduce_fusion.1
  59.6 0.2 fusion.17
  59.8 2.8 %fusion.12 = f32[512,1920]{0,1:T(8,128)} fusion(bf16[256,1920]{1,0:T(8,128)(2,1)S(1)} %reshape.120, pred[256]{0:T(512)(128)(4,1)S(1)} %le.31, bf16[256,512]{1,0:T(8,128)(2,1)S(1)} %get-tuple-element.6, f32[512]{0:T(512)S(1)} %bitcast.25, f32[512]{0:T(512)S(1)} %bitcast.23, f32[256]{0:T(256)S(1)} %add_rsqrt_fusion.1, f32[256]{0:T(256)S(1)} %broadcast_multiply_fusion.1), kind=kOutput, calls=%fused_computation.26 | convolution fusion | flops 504594432 | bytes 5183744 | tf_op jit(solution)/shard_map/dot_general | solution.py:99
  62.6 0.0 copy-start.3
  62.6 0.0 copy-start.4
  62.6 0.0 copy-start.1
  62.6 0.0 reduce-scatter.2.cloned.1.call-update
  62.6 0.6 copy-done.3
  63.2 0.6 fusion.41
  64.5 0.0 copy-done.4
  64.5 0.3 dynamic-update-slice
  64.7 10.8 %all-reduce = bf16[1920]{0:T(1024)(128)(2,1)S(1)} all-reduce(bf16[1920]{0:T(1024)(128)(2,1)S(1)} %dynamic-update-slice), channel_id=1, replica_groups=mesh['dp'=8,'fsdp'=4] {'fsdp'}, use_global_device_ids=true, to_apply=%add | all-reduce | flops 1920 | bytes 7680
  76.2 0.0 copy-done.1
  76.2 0.6 convert_reduce_fusion
  76.8 7.7 %all-reduce.1 = f32[1920]{0:T(1024)S(1)} all-reduce(f32[1920]{0:T(1024)S(1)} %convert_reduce_fusion), channel_id=3, replica_groups=mesh['dp'=8,'fsdp'=4] {'fsdp'}, use_global_device_ids=true, to_apply=%region_11.12.clone | all-reduce | flops 1920 | bytes 15360
  84.5 0.1 dynamic-slice.2
  84.6 0.0 all-gather.2.cloned.1.call-done
  84.6 2.3 %fusion.1 = bf16[256,1920]{1,0:T(8,128)(2,1)S(1)} fusion(bf16[512,1920]{0,1:T(8,128)(2,1)} %all-gather.2.cloned.1.call-done, f32[256]{0:T(256)S(1)} %convert_element_type.50, f32[1920]{0:T(1024)S(1)} %convert_element_type.49, bf16[256,512]{1,0:T(8,128)(2,1)S(1)} %get-tuple-element.6, f32[512]{0:T(512)S(1)} %bitcast.26, f32[512]{0:T(512)S(1)} %bitcast.24, ...), kind=kOutput, calls=%fused_computation.2 | convolution fusion | flops 505577472 | bytes 3226112 | tf_op jit(solution)/shard_map/dot_general | solution.py:93
  87.0 1.2 reshape.119
  88.1 48.4 %reduce-scatter.2.cloned.1.call-done = f32[512,480]{0,1:T(8,128)} async-done(((f32[512,1920]{0,1:T(8,128)}), f32[512,480]{0,1:T(8,128)}) %reduce-scatter.2.cloned.1.call-update) | async-done | bytes 983056 | tf_op jit(solution)/shard_map/reduce_scatter | solution.py:104
  136.6 34.2 %all-reduce.4 = (bf16[512,480]{0,1:T(8,128)(2,1)}, bf16[480]{0:T(512)(128)(2,1)}) all-reduce(f32[512,480]{0,1:T(8,128)} %reduce-scatter.2.cloned.1.call-done, f32[480]{0:T(512)S(1)} %dynamic-slice.2), channel_id=1, replica_groups=mesh['dp'=8,'fsdp'=4] {'dp'}, use_global_device_ids=true, to_apply=%region_9.10 | all-reduce | flops 246240 | bytes 1477440 | tf_op jit(solution)/shard_map/psum | solution.py:107
  (12 shorter events, 0.1 us)
Async XLA Ops:
  7.2 49.0 %copy-start = (bf16[1536,512]{1,0:T(8,128)(2,1)S(1)}, bf16[1536,512]{1,0:T(8,128)(2,1)}, u32[]{:S(2)}) copy-start(bf16[1536,512]{1,0:T(8,128)(2,1)} %param.14) | copy-start | bytes 4718596
  10.2 11.0 %all-to-all-start.1 = ((s32[8,1,8]{2,1,0:T(1,128)}), s32[8,1,8]{2,1,0:T(1,128)S(1)}, u32[]{:S(2)}, u32[]{:S(2)}) async-start(s32[8,1,8]{2,1,0:T(1,128)} %bitcast.9), calls=%async_computation.1 | async-start | bytes 8192 | tf_op jit(solution)/shard_map/all_to_all | solution.py:81
  15.5 69.2 %all-gather.2.cloned.1.call-start = ((), (), s32[]{:S(2)}) async-start(), calls=%async_computation.3 | async-start | bytes 2457600 | tf_op jit(solution)/shard_map/all_gather | solution.py:62
  19.5 10.8 %copy-start.2 = (bf16[10,512]{1,0:T(8,128)(2,1)S(1)}, bf16[10,512]{1,0:T(8,128)(2,1)}, u32[]{:S(2)}) copy-start(bf16[10,512]{1,0:T(8,128)(2,1)} %param.13) | copy-start | bytes 30724
  21.3 8.2 %all-to-all-start = ((bf16[8,2,200]{2,1,0:T(2,128)(2,1)}), bf16[8,2,200]{2,1,0:T(2,128)(2,1)S(1)}, u32[]{:S(2)}, u32[]{:S(2)}) async-start(bf16[8,2,200]{2,1,0:T(2,128)(2,1)} %reshape.136), calls=%async_computation | async-start | bytes 16384 | tf_op jit(solution)/shard_map/all_to_all | solution.py:78
  25.5 111.1 %reduce-scatter.2.cloned.1.call-start = ((), (), s32[]{:S(2)}) async-start(), calls=%async_computation.4 | async-start | bytes 4915200 | tf_op jit(solution)/shard_map/reduce_scatter | solution.py:104
  62.6 0.7 copy-start.3
  62.6 1.9 %copy-start.4 = (bf16[480]{0:T(512)(128)(2,1)S(1)}, bf16[480]{0:T(512)(128)(2,1)}, u32[]{:S(2)}) copy-start(bf16[480]{0:T(512)(128)(2,1)} %param.18) | copy-start | bytes 2884
  62.6 13.7 %copy-start.1 = (bf16[64,4,1920]{2,1,0:T(4,128)(2,1)S(1)}, bf16[64,4,1920]{2,1,0:T(4,128)(2,1)}, u32[]{:S(2)}) copy-start(bf16[64,4,1920]{2,1,0:T(4,128)(2,1)} %param.19) | copy-start | bytes 2949124
Sparse Core Ops, SparseCore 0:
  17.9 44.6 all-gather.1
  64.8 71.7 reduce-scatter.1
where the time goes:
time: 181 us; the launch traced here: 178 us
  blocking collectives  52.7 us (29%)
  waiting for transfers between devices  51.7 us (29%)
  local copies, waits for them, and re-layouts  29.3 us (16%)
  between operations  15.5 us (9%)
  other arithmetic  10.7 us (6%)
  starting transfers between devices  9.44 us (5%)
  matrix products  8.21 us (5%)
    reduce_scatter x1, waiting for transfers between devices, local(): lax.psum_scatter(weight_term, 'fsdp', scatter_dimension=1, tiled=True)  48.4 us
    psum x1, blocking collectives, local(): grad_weight, grad_bias = lax.psum((part_weight, part_bias), 'dp')  34.2 us
    unnamed x2, blocking collectives  18.5 us
    slice x1, local copies, waits for them, and re-layouts, encode(): first_conv[:, 2:2 * frame_count + 2:2]  6.05 us
    slice x1, local copies, waits for them, and re-layouts, encode(): first_conv[:, 1:2 * frame_count + 1:2]  5.99 us
    slice x1, local copies, waits for them, and re-layouts, encode(): first_conv[:, 0:2 * frame_count:2]  5.98 us
    all_to_all x1, starting transfers between devices, local(): lax.all_to_all(slot_length.reshape(dp_size, slot_cap), 'dp', split_axis=0...  5.22 us
    all_to_all x1, starting transfers between devices, local(): lax.all_to_all(slot_wave.reshape(dp_size, slot_cap, -1), 'dp', split_axis...  4.21 us
  transfers between devices with their start and end apart: 4, of which 2 were waited for; matrix products, arithmetic and copies ran while one was open for 25% of the time, Pallas kernels for 0%

commit v1 on v0

--- a/solution.py
+++ b/solution.py
@@ -1,7 +1,324 @@
+import functools
+import math
+
 import jax
 import jax.numpy as jnp
 from jax import lax
+from jax.experimental import pallas as pl
+from jax.experimental.pallas import tpu as pltpu
 from jax.sharding import PartitionSpec as P
+
+MESH = pl.DeviceIdType.MESH
+F32 = jnp.float32
+BF16 = jnp.bfloat16
+
+
+def gelu(v):
+    return 0.5 * v * (1.0 + lax.erf(v * (1.0 / math.sqrt(2.0))))
+
+
+def norm_rows(values, gain_vec, bias_vec):
+    avg = jnp.mean(values, axis=-1, keepdims=True)
+    centred = values - avg
+    var = jnp.mean(centred * centred, axis=-1, keepdims=True)
+    return centred * lax.rsqrt(var + 1e-05) * gain_vec + bias_vec
+
+
+def dot_t(a, b):
+    return lax.dot_general(a, b, (((0,), (0,)), ((), ())), preferred_element_type=F32)
+
+
+def fused(
+    samp, n_dp, n_f, cap, frames,
+    data_ref, w0_ref, w1_ref, gain_ref, nbias_ref, pw_ref, pb_ref, cot_ref,
+    feat_ref, gw_ref, gb_ref,
+    xsend, xrecv, w0p, wfull, pbfull, cotb, normed_ref, masked_ref, mask_ref,
+    asend, arecv, gown, bsend, brecv, csend, crecv, gwbuf,
+    hsend, hrecv, hsum, hall,
+    x_s, x_r, wz_s, wz_r, wp_s, wp_r, wm_s, wm_r, pb_s, pb_r,
+    a_s, a_r, b_s, b_r, c_s, c_r, d_s, d_r, e_s, e_r, h_s, h_r, k_s, k_r,
+):
+    d = lax.axis_index("dp")
+    f = lax.axis_index("fsdp")
+    core = d % 2
+    chip = d // 2
+    cx = chip % 2
+    cy = chip // 2
+    n_chip = n_dp // 2
+    depth = pw_ref.shape[0]
+    cols = pw_ref.shape[1]
+    half = depth // 2
+    ch = half // n_chip
+    slots = n_dp * cap
+    mate = chip * 2 + (1 - core)
+
+    def other(c):
+        return ((cy + c // 2) % 2) * 2 + (cx + c % 2) % 2
+
+    def copy(src, dst, s_sem, r_sem, dd, ff):
+        return pltpu.make_async_remote_copy(
+            src_ref=src, dst_ref=dst, send_sem=s_sem, recv_sem=r_sem,
+            device_id=(dd, ff), device_id_type=MESH,
+        )
+
+    barrier = pltpu.get_barrier_semaphore()
+    for o in range(1, n_dp):
+        pl.semaphore_signal(barrier, inc=1, device_id=((d + o) % n_dp, f), device_id_type=MESH)
+    for o in range(1, n_f):
+        pl.semaphore_signal(barrier, inc=1, device_id=(d, (f + o) % n_f), device_id_type=MESH)
+
+    rows = data_ref.shape[0]
+    table = data_ref[...]
+    target = table[:, samp + 1 : samp + 2].astype(F32)
+    lane = lax.broadcasted_iota(jnp.int32, (rows, 128), 1).astype(F32)
+    named = (target == lane).astype(F32)
+    tri_r = lax.broadcasted_iota(jnp.int32, (rows, rows), 0)
+    tri_c = lax.broadcasted_iota(jnp.int32, (rows, rows), 1)
+    earlier = (tri_c < tri_r).astype(F32).astype(BF16)
+    before = jnp.dot(earlier, named.astype(BF16), preferred_element_type=F32)
+    rank = jnp.sum(before * named, axis=1, keepdims=True)
+    place = target * cap + rank
+    placing = (place == lane).astype(F32).astype(BF16)
+    placed = dot_t(placing, table)[:slots]
+    xsend[...] = placed.reshape(n_dp, cap, 128)
+    wfull[f] = pw_ref[...]
+    pbfull[f] = jnp.broadcast_to(pb_ref[...].astype(F32), (8, cols))
+    pl.semaphore_wait(barrier, n_dp + n_f - 2)
+
+    x_cp = []
+    for o in range(1, n_dp):
+        p = (d + o) % n_dp
+        x_cp.append(copy(xsend.at[p], xrecv.at[d], x_s.at[o], x_r.at[o], p, f))
+        x_cp[-1].start()
+    mine = core * half + chip * ch
+    z_cp, pb_cp = [], []
+    for o in range(1, n_f):
+        p = (f + o) % n_f
+        z_cp.append(copy(
+            wfull.at[f, pl.ds(mine, ch)], wfull.at[f, pl.ds(mine, ch)],
+            wz_s.at[o], wz_r.at[o], d, p))
+        z_cp[-1].start()
+        pb_cp.append(copy(pbfull.at[f], pbfull.at[f], pb_s.at[o], pb_r.at[o], d, p))
+        pb_cp[-1].start()
+    xrecv[d] = xsend[d]
+    w0p[...] = jnp.zeros_like(w0p)
+    w0p[0 : w0_ref.shape[0], :] = w0_ref[...]
+    for b in range(n_f):
+        cotb[b] = cot_ref[:, b * cols : (b + 1) * cols]
+    for o in range(1, n_dp):
+        q = (d + n_dp - o) % n_dp
+        copy(xsend.at[q], xrecv.at[q], x_s.at[o], x_r.at[o], q, f).wait_recv()
+
+    x = xrecv[...].reshape(slots, 128)
+    length = x[:, samp : samp + 1]
+    first = []
+    for t in range(2 * frames + 1):
+        xt = x if t == 0 else pltpu.roll(x, 128 - 5 * t, axis=1)
+        v = jnp.dot(xt.astype(BF16), w0p[...], preferred_element_type=F32)
+        first.append(gelu(norm_rows(v, gain_ref[0:1], nbias_ref[0:1])).astype(BF16))
+
+    p_cp = []
+    for o in range(1, n_f):
+        q = (f + n_f - o) % n_f
+        part = wfull.at[q, pl.ds(mine, ch)]
+        copy(part, part, wz_s.at[o], wz_r.at[o], d, q).wait_recv()
+        for c in range(1, n_chip):
+            i = o * n_chip + c
+            p_cp.append(copy(part, part, wp_s.at[i], wp_r.at[i], other(c) * 2 + core, f))
+            p_cp[-1].start()
+
+    normed, masked, masks = [], [], []
+    for j in range(frames):
+        taps = jnp.concatenate(first[2 * j : 2 * j + 3], axis=1)
+        v = jnp.dot(taps, w1_ref[...], preferred_element_type=F32)
+        hid = gelu(norm_rows(v, gain_ref[1:2], nbias_ref[1:2])).astype(BF16).astype(F32)
+        nj = norm_rows(hid, gain_ref[2:3], nbias_ref[2:3]).astype(BF16)
+        mj = (length >= 10.0 * j + 20.0).astype(F32)
+        normed.append(nj)
+        masks.append(jnp.broadcast_to(mj, (slots, 128)).astype(BF16))
+    total = slots * frames
+    pr = lax.broadcasted_iota(jnp.int32, (total, total), 0)
+    pc = lax.broadcasted_iota(jnp.int32, (total, total), 1)
+    perm = ((pr % frames) * slots + pr // frames == pc).astype(F32).astype(BF16)
+    nrm = jnp.dot(perm, jnp.concatenate(normed, axis=0), preferred_element_type=F32)
+    msk = jnp.dot(perm, jnp.concatenate(masks, axis=0), preferred_element_type=F32)
+    normed_ref[...] = nrm.astype(BF16)
+    masked_ref[...] = (nrm * msk[:, 0:1]).astype(BF16)
+    mask_ref[...] = msk
+
+    order = [o % n_f for o in range(1, n_f + 1)]
+    a_cp = []
+    theirs = masked_ref[:, pl.ds(pl.multiple_of((1 - core) * half, half), half)]
+    for o in order:
+        b = (f + o) % n_f
+        asend[o] = dot_t(theirs, cotb[b]).astype(BF16)
+        a_cp.append(copy(asend.at[o], arecv.at[o], a_s.at[o], a_r.at[o], mate, f))
+        a_cp[-1].start()
+    ours = masked_ref[:, pl.ds(pl.multiple_of(core * half, half), half)]
+    for o in order:
+        b = (f + o) % n_f
+        gown[o] = dot_t(ours, cotb[b])
+    h_cp = []
+    ones = mask_ref[...].astype(BF16)
+    for o in order:
+        b = (f + o) % n_f
+        hsend[o] = dot_t(ones, cotb[b])[0:8]
+        if o:
+            h_cp.append(copy(hsend.at[o], hrecv.at[o], h_s.at[o], h_r.at[o], d, b))
+            h_cp[-1].start()
+
+    b_cp = []
+    for o in order:
+        copy(asend.at[o], arecv.at[o], a_s.at[o], a_r.at[o], mate, f).wait_recv()
+        both = gown[o] + arecv[o].astype(F32)
+        gown[o] = both
+        bsend[o] = both.astype(BF16)
+        for c in range(1, n_chip):
+            to = other(c)
+            i = o * n_chip + c
+            b_cp.append(copy(
+                bsend.at[o, pl.ds(to * ch, ch)], brecv.at[i],
+                b_s.at[i], b_r.at[i], to * 2 + core, f))
+            b_cp[-1].start()
+
+    m_cp = []
+    for o in range(1, n_f):
+        q = (f + n_f - o) % n_f
+        for c in range(1, n_chip):
+            i = o * n_chip + c
+            theirs_at = core * half + other(c) * ch
+            part = wfull.at[q, pl.ds(theirs_at, ch)]
+            copy(part, part, wp_s.at[i], wp_r.at[i], other(c) * 2 + core, f).wait_recv()
+        block = wfull.at[q, pl.ds(core * half, half)]
+        m_cp.append(copy(block, block, wm_s.at[o], wm_r.at[o], mate, f))
+        m_cp[-1].start()
+        copy(pbfull.at[q], pbfull.at[q], pb_s.at[o], pb_r.at[o], d, q).wait_recv()
+    for o in range(1, n_f):
+        q = (f + n_f - o) % n_f
+        block = wfull.at[q, pl.ds((1 - core) * half, half)]
+        copy(block, block, wm_s.at[o], wm_r.at[o], mate, f).wait_recv()
+    for b in range(n_f):
+        v = jnp.dot(normed_ref[...], wfull[b], preferred_element_type=F32) + pbfull[b][0:1]
+        feat_ref[:, b * cols : (b + 1) * cols] = (v * mask_ref[:, 0:1]).astype(BF16)
+
+    c_cp = []
+    own = None
+    for o in order:
+        part = gown[o, pl.ds(chip * ch, ch), :]
+        for c in range(1, n_chip):
+            i = o * n_chip + c
+            copy(brecv.at[i], brecv.at[i], b_s.at[i], b_r.at[i], other(c) * 2 + core, f).wait_recv()
+            part = part + brecv[i].astype(F32)
+        if o:
+            csend[o] = part.astype(BF16)
+            c_cp.append(copy(csend.at[o], crecv.at[o], c_s.at[o], c_r.at[o], d, (f + o) % n_f))
+            c_cp[-1].start()
+        else:
+            own = part
+    hown = hsend[0]
+    for o in range(1, n_f):
+        q = (f + n_f - o) % n_f
+        copy(hsend.at[o], hrecv.at[o], h_s.at[o], h_r.at[o], d, q).wait_recv()
+        hown = hown + hrecv[o]
+    hsum[...] = hown
+    k_cp = []
+    for o in range(1, n_dp):
+        k_cp.append(copy(hsum, hall.at[o], k_s.at[o], k_r.at[o], (d + o) % n_dp, f))
+        k_cp[-1].start()
+    for o in range(1, n_f):
+        q = (f + n_f - o) % n_f
+        copy(csend.at[o], crecv.at[o], c_s.at[o], c_r.at[o], d, q).wait_recv()
+        own = own + crecv[o].astype(F32)
+    gwbuf[pl.ds(mine, ch), :] = own.astype(BF16)
+
+    d_cp = []
+    src = gwbuf.at[pl.ds(mine, ch)]
+    for c in range(1, n_chip):
+        d_cp.append(copy(src, src, d_s.at[c], d_r.at[c], other(c) * 2 + core, f))
+        d_cp[-1].start()
+    e_cp = [copy(src, src, e_s.at[0], e_r.at[0], mate, f)]
+    e_cp[0].start()
+    for c in range(1, n_chip):
+        part = gwbuf.at[pl.ds(core * half + other(c) * ch, ch)]
+        copy(part, part, d_s.at[c], d_r.at[c], other(c) * 2 + core, f).wait_recv()
+        e_cp.append(copy(part, part, e_s.at[c], e_r.at[c], mate, f))
+        e_cp[-1].start()
+    for o in range(1, n_dp):
+        copy(hsum, hall.at[o], k_s.at[o], k_r.at[o], (d + n_dp - o) % n_dp, f).wait_recv()
+        hown = hown + hall[o]
+    gb_ref[...] = hown[0:1].astype(BF16)
+    for c in range(n_chip):
+        at = other(c) if c else chip
+        part = gwbuf.at[pl.ds((1 - core) * half + at * ch, ch)]
+        copy(part, part, e_s.at[c], e_r.at[c], mate, f).wait_recv()
+    gw_ref[...] = gwbuf[...]
+    for one in x_cp + z_cp + pb_cp + p_cp + m_cp + a_cp + h_cp + b_cp + c_cp + k_cp + d_cp + e_cp:
+        one.wait_send()
+
+
+def local_fused(
+    waveform, destination, lengths, conv0_weight, conv1_weight,
+    norm_gain, norm_bias, proj_weight, proj_bias, cotangent,
+):
+    n_dp, n_f = lax.axis_size("dp"), lax.axis_size("fsdp")
+    rows, samp = waveform.shape
+    slots, frames, width = cotangent.shape
+    cap = slots // n_dp
+    depth, cols = proj_weight.shape
+    n_chip, half = n_dp // 2, depth // 2
+    ch = half // n_chip
+    total = slots * frames
+    data = jnp.concatenate(
+        [waveform, lengths[:, None].astype(BF16), destination.astype(BF16),
+         jnp.zeros((rows, 128 - samp - 2), BF16)], axis=1)
+    vmem = pl.BlockSpec(memory_space=pltpu.VMEM)
+    dma = lambda n: pltpu.SemaphoreType.DMA((n,))
+    nc = n_f * n_chip
+    feats, gw, gb = pl.pallas_call(
+        functools.partial(fused, samp, n_dp, n_f, cap, frames),
+        out_shape=(
+            jax.ShapeDtypeStruct((total, width), BF16),
+            jax.ShapeDtypeStruct((depth, cols), BF16),
+            jax.ShapeDtypeStruct((1, cols), BF16),
+        ),
+        in_specs=[vmem] * 8,
+        out_specs=(vmem,) * 3,
+        scratch_shapes=[
+            pltpu.VMEM((n_dp, cap, 128), F32),
+            pltpu.VMEM((n_dp, cap, 128), F32),
+            pltpu.VMEM((128, depth), BF16),
+            pltpu.VMEM((n_f, depth, cols), BF16),
+            pltpu.VMEM((n_f, 8, cols), F32),
+            pltpu.VMEM((n_f, total, cols), BF16),
+            pltpu.VMEM((total, depth), BF16),
+            pltpu.VMEM((total, depth), BF16),
+            pltpu.VMEM((total, 128), F32),
+            pltpu.VMEM((n_f, half, cols), BF16),
+            pltpu.VMEM((n_f, half, cols), BF16),
+            pltpu.VMEM((n_f, half, cols), F32),
+            pltpu.VMEM((n_f, half, cols), BF16),
+            pltpu.VMEM((nc, ch, cols), BF16),
+            pltpu.VMEM((n_f, ch, cols), BF16),
+            pltpu.VMEM((n_f, ch, cols), BF16),
+            pltpu.VMEM((depth, cols), BF16),
+            pltpu.VMEM((n_f, 8, cols), F32),
+            pltpu.VMEM((n_f, 8, cols), F32),
+            pltpu.VMEM((8, cols), F32),
+            pltpu.VMEM((n_dp, 8, cols), F32),
+            dma(n_dp), dma(n_dp), dma(n_f), dma(n_f), dma(nc), dma(nc),
+            dma(n_f), dma(n_f), dma(n_f), dma(n_f),
+            dma(n_f), dma(n_f), dma(nc), dma(nc), dma(n_f), dma(n_f),
+            dma(n_chip), dma(n_chip), dma(n_chip), dma(n_chip),
+            dma(n_f), dma(n_f), dma(n_dp), dma(n_dp),
+        ],
+        compiler_params=pltpu.CompilerParams(
+            collective_id=0, has_side_effects=True, vmem_limit_bytes=48 * 1024 * 1024),
+        cost_estimate=pl.CostEstimate(
+            flops=2 * total * depth * (3 * depth + 2 * width),
+            bytes_accessed=8 * depth * width, transcendentals=13 * slots * depth),
+    )(data, conv0_weight, conv1_weight, norm_gain, norm_bias, proj_weight,
+      proj_bias[None, :], cotangent.reshape(total, width))
+    return feats.reshape(slots, frames, width), gw, gb[0]
 
 
 def layer_norm(values, gain_vec, bias_vec):
@@ -122,4 +439,5 @@
         P(("dp", "fsdp"), None, None),
     )
     out_specs = (P(("dp", "fsdp"), None, None), P(None, "fsdp"), P("fsdp"))
-    return jax.shard_map(local, mesh=mesh, in_specs=in_specs, out_specs=out_specs, check_vma=False)
+    body = local_fused if (mesh.shape["dp"], mesh.shape["fsdp"]) == (8, 4) else local
+    return jax.shard_map(body, mesh=mesh, in_specs=in_specs, out_specs=out_specs, check_vma=False)

time: 181 us -> 49.6 us (0.27); the launches traced: 178 us -> 49.4 us
  blocking collectives: 52.7 us -> 0 us
  waiting for transfers between devices: 51.7 us -> 0 us
  Pallas kernels: 0 us -> 39.9 us
  local copies, waits for them, and re-layouts: 29.3 us -> 5.99 us
  between operations: 15.5 us -> 0.73 us
  starting transfers between devices: 9.44 us -> 0 us
  matrix products: 8.21 us -> 0 us
  other arithmetic: 10.7 us -> 2.76 us
    reduce_scatter x1 -> x0, waiting for transfers between devices: 48.4 us -> none  [local(): lax.psum_scatter(weight_term, 'fsdp', scatter_dimension=1, tiled=True)]
    pallas_call x0 -> x1, Pallas kernels: none -> 39.9 us  [local_fused(): pl.pallas_call(functools.partial(fused, samp, n_dp, n_f, cap, frames), ou...]
    psum x1 -> x0, blocking collectives: 34.2 us -> none  [local(): grad_weight, grad_bias = lax.psum((part_weight, part_bias), 'dp')]
    slice x6 -> x0, local copies, waits for them, and re-layouts: 19.7 us -> none  [the longest x1 6.05 us: encode(): first_conv[:, 2:2 * frame_count + 2:2]]
    unnamed x2 -> x0, blocking collectives: 18.5 us -> none
    all_to_all x2 -> x0, starting transfers between devices: 9.43 us -> none  [the longest x1 5.22 us: local(): lax.all_to_all(slot_length.reshape(dp_size, slot_cap), 'dp', split_axis=0...]
    dot_general x5 -> x0, matrix products: 8.21 us -> none  [the longest x1 2.77 us: local(): lax.dot_general(normed, grad_out, (((0,), (0,)), ((), ())), preferred_ele...]
    reduce_sum x7 -> x0, other arithmetic: 4.43 us -> none  [the longest x1 1.41 us: layer_norm(): avg_value = jnp.mean(values, axis=-1, keepdims=True)]
  transfers between devices with their start and end apart: 4 -> 0, of which waited for: 2 -> 0; matrix products, arithmetic and copies ran while one was open for 25% -> 0% of each run, Pallas kernels for 0% -> 0%
where the time goes in v1:
time: 49.6 us; the launch traced here: 49.4 us
  Pallas kernels  39.9 us (80%)
  local copies, waits for them, and re-layouts  5.99 us (12%)
  other arithmetic  2.76 us (6%)
  between operations  0.73 us (1%)
    pallas_call x1, Pallas kernels, local_fused(): pl.pallas_call(functools.partial(fused, samp, n_dp, n_f, cap, frames), ou...  39.9 us
    unnamed x12, local copies, waits for them, and re-layouts  3.64 us
    reshape x1, local copies, waits for them, and re-layouts, local_fused(): return (feats.reshape(slots, frames, width), gw, gb[0])  1.17 us

profile of v1, /device:TPU:1, one launch (start us, length us, event | category | flops | bytes accessed | tf_op | source)
XLA Modules:
  0.0 49.4 jit_solution(13115281722948879772)
XLA Ops:
  0.6 0.0 copy-start.4
  0.6 0.0 copy-start.3
  0.7 0.0 copy-start.2
  0.7 0.0 copy-start.1
  0.7 0.7 %convert_element_type.11 = bf16[32,1]{0,1:T(2,128)(2,1)S(1)} convert(s32[32,1]{0,1:T(1,128)} %param.11) | non-fusion elementwise | flops 32 | bytes 192 | tf_op jit(solution)/shard_map/convert_element_type | solution.py:272
  1.4 0.7 %convert_bitcast_fusion = bf16[32,1]{0,1:T(2,128)(2,1)S(1)} fusion(s32[32]{0:T(128)} %param.12), kind=kLoop, calls=%fused_computation.1 | loop fusion | flops 32 | bytes 192 | tf_op jit(solution)/shard_map/convert_element_type | solution.py:272
  2.1 0.1 pad.3.clone
  2.1 0.7 %broadcast_in_dim.8.pb_ref = bf16[1,480]{1,0:T(2,128)(2,1)S(1)} reshape(bf16[480]{0:T(512)(128)(2,1)} %param.18) | data formatting | bytes 1920 | tf_op jit(solution)/shard_map/broadcast_in_dim | solution.py:320
  2.8 0.1 copy.13
  2.9 0.1 copy.14
  3.0 0.8 %maximum_maximum_fusion.data_ref = bf16[32,128]{1,0:T(8,128)(2,1)S(1)} fusion(bf16[32,1]{1,0:T(8,128)(2,1)S(1)} %copy.14, bf16[32,1]{1,0:T(8,128)(2,1)S(1)} %copy.13, bf16[32,50]{1,0:T(8,128)(2,1)} %param.10, bf16[128]{0:T(256)(128)(2,1)S(1)} %pad.3.clone), kind=kLoop, calls=%fused_computation | loop fusion | flops 32768 | bytes 11776 | tf_op jit(solution)/shard_map/concatenate | solution.py:271
  3.8 1.2 %copy.15.pw_ref = bf16[512,480]{1,0:T(8,128)(2,1)S(1)} copy(bf16[512,480]{0,1:T(8,128)(2,1)} %param.17) | data formatting | bytes 983040 | tf_op args[7]
  5.1 0.0 copy-done.4
  5.1 0.2 reshape.13.cot_ref
  5.3 0.0 copy-done.3
  5.3 0.0 copy-done.2
  5.3 0.0 copy-done.1
  5.3 0.0 copy-start
  5.3 1.4 %copy-done = bf16[1536,512]{1,0:T(8,128)(2,1)S(1)} copy-done((bf16[1536,512]{1,0:T(8,128)(2,1)S(1)}, bf16[1536,512]{1,0:T(8,128)(2,1)}, u32[]{:S(2)}) %copy-start) | copy-done | bytes 1572888
  6.7 39.9 %shard_map.121 = (bf16[256,1920]{1,0:T(8,128)(2,1)S(1)}, bf16[512,480]{1,0:T(8,128)(2,1)S(1)}, bf16[1,480]{1,0:T(2,128)(2,1)S(1)}) custom-call(bf16[32,128]{1,0:T(8,128)(2,1)S(1)} %maximum_maximum_fusion.data_ref, bf16[10,512]{1,0:T(8,128)(2,1)S(1)} %copy-done.1, bf16[1536,512]{1,0:T(8,128)(2,1)S(1)} %copy-done, f32[3,512]{1,0:T(4,128)S(1)} %copy-done.2, ...), custom_call_target="tpu_custom_call" | custom-call | flops 1409286144 | bytes 7864320 | tf_op jit(solution)/shard_map/pallas_call | solution.py:277
  46.6 1.2 %reshape.14 = bf16[64,4,1920]{2,1,0:T(4,128)(2,1)} reshape(bf16[256,1920]{1,0:T(8,128)(2,1)S(1)} %get-tuple-element.6) | data formatting | bytes 1966080 | tf_op jit(solution)/shard_map/reshape | solution.py:321
  47.8 0.6 %reduce = bf16[480]{0:T(512)(128)(2,1)} reduce(bf16[1,480]{1,0:T(2,128)(2,1)S(1)} %get-tuple-element.8, bf16[]{:T(256)} %constant.2), dimensions={0}, to_apply=%get-tuple-element.8.reduce_sub_computation | reduce | bytes 1922 | tf_op jit(solution)/shard_map/pallas_call | solution.py:277
  48.4 1.0 %copy.16 = bf16[512,480]{0,1:T(8,128)(2,1)} copy(bf16[512,480]{1,0:T(8,128)(2,1)S(1)} %get-tuple-element.10) | data formatting | bytes 983040
  (1 shorter events, 0.0 us)
Async XLA Ops:
  0.6 4.4 %copy-start.4 = (bf16[64,4,1920]{2,1,0:T(4,128)(2,1)S(1)}, bf16[64,4,1920]{2,1,0:T(4,128)(2,1)}, u32[]{:S(2)}) copy-start(bf16[64,4,1920]{2,1,0:T(4,128)(2,1)} %param.19) | copy-start | bytes 2949124
  0.6 4.7 %copy-start.3 = (f32[3,512]{1,0:T(4,128)S(1)}, f32[3,512]{1,0:T(4,128)}, u32[]{:S(2)}) copy-start(f32[3,512]{1,0:T(4,128)} %nbias_ref.1) | copy-start | bytes 18436
  0.7 4.7 %copy-start.2 = (f32[3,512]{1,0:T(4,128)S(1)}, f32[3,512]{1,0:T(4,128)}, u32[]{:S(2)}) copy-start(f32[3,512]{1,0:T(4,128)} %gain_ref.1) | copy-start | bytes 18436
  0.7 4.7 %copy-start.1 = (bf16[10,512]{1,0:T(8,128)(2,1)S(1)}, bf16[10,512]{1,0:T(8,128)(2,1)}, u32[]{:S(2)}) copy-start(bf16[10,512]{1,0:T(8,128)(2,1)} %w0_ref.1) | copy-start | bytes 30724
  5.3 1.4 %copy-start = (bf16[1536,512]{1,0:T(8,128)(2,1)S(1)}, bf16[1536,512]{1,0:T(8,128)(2,1)}, u32[]{:S(2)}) copy-start(bf16[1536,512]{1,0:T(8,128)(2,1)} %w1_ref.1) | copy-start | bytes 4718596

commit v2 on v1

--- a/solution.py
+++ b/solution.py
@@ -30,9 +30,9 @@
 
 def fused(
     samp, n_dp, n_f, cap, frames,
-    data_ref, w0_ref, w1_ref, gain_ref, nbias_ref, pw_ref, pb_ref, cot_ref,
+    wave_ref, dest_ref, len_ref, w0_ref, w1_hbm, gain_ref, nbias_ref, pw_ref, pb_ref, cot_ref,
     feat_ref, gw_ref, gb_ref,
-    xsend, xrecv, w0p, wfull, pbfull, cotb, normed_ref, masked_ref, mask_ref,
+    w1_ref, w1_sem, table_ref, xsend, xrecv, w0p, wfull, pbfull, cotb, normed_ref, masked_ref, mask_ref,
     asend, arecv, gown, bsend, brecv, csend, crecv, gwbuf,
     hsend, hrecv, hsum, hall,
     x_s, x_r, wz_s, wz_r, wp_s, wp_r, wm_s, wm_r, pb_s, pb_r,
@@ -45,8 +45,7 @@
     cx = chip % 2
     cy = chip // 2
     n_chip = n_dp // 2
-    depth = pw_ref.shape[0]
-    cols = pw_ref.shape[1]
+    cols, depth = pw_ref.shape
     half = depth // 2
     ch = half // n_chip
     slots = n_dp * cap
@@ -61,19 +60,26 @@
             device_id=(dd, ff), device_id_type=MESH,
         )
 
+    w1_cp = pltpu.make_async_copy(w1_hbm, w1_ref, w1_sem)
+    w1_cp.start()
     barrier = pltpu.get_barrier_semaphore()
     for o in range(1, n_dp):
         pl.semaphore_signal(barrier, inc=1, device_id=((d + o) % n_dp, f), device_id_type=MESH)
     for o in range(1, n_f):
         pl.semaphore_signal(barrier, inc=1, device_id=(d, (f + o) % n_f), device_id_type=MESH)
 
-    rows = data_ref.shape[0]
-    table = data_ref[...]
-    target = table[:, samp + 1 : samp + 2].astype(F32)
-    lane = lax.broadcasted_iota(jnp.int32, (rows, 128), 1).astype(F32)
-    named = (target == lane).astype(F32)
+    rows = wave_ref.shape[0]
     tri_r = lax.broadcasted_iota(jnp.int32, (rows, rows), 0)
     tri_c = lax.broadcasted_iota(jnp.int32, (rows, rows), 1)
+    lane = lax.broadcasted_iota(jnp.int32, (rows, 128), 1)
+    spread = jnp.broadcast_to(len_ref[...].astype(F32), (rows, rows))
+    span = jnp.sum(jnp.where(tri_r == tri_c, spread, 0.0), axis=1, keepdims=True)
+    table_ref[...] = jnp.where(lane == samp, span, 0.0).astype(BF16)
+    table_ref[:, 0:samp] = wave_ref[...]
+    table = table_ref[...]
+    lane = lane.astype(F32)
+    target = dest_ref[...].astype(F32)
+    named = (target == lane).astype(F32)
     earlier = (tri_c < tri_r).astype(F32).astype(BF16)
     before = jnp.dot(earlier, named.astype(BF16), preferred_element_type=F32)
     rank = jnp.sum(before * named, axis=1, keepdims=True)
@@ -81,8 +87,12 @@
     placing = (place == lane).astype(F32).astype(BF16)
     placed = dot_t(placing, table)[:slots]
     xsend[...] = placed.reshape(n_dp, cap, 128)
-    wfull[f] = pw_ref[...]
-    pbfull[f] = jnp.broadcast_to(pb_ref[...].astype(F32), (8, cols))
+    eye_r = lax.broadcasted_iota(jnp.int32, (depth, depth), 0)
+    eye_c = lax.broadcasted_iota(jnp.int32, (depth, depth), 1)
+    eye = (eye_r == eye_c).astype(F32).astype(BF16)
+    wfull[f] = lax.dot_general(
+        eye, pw_ref[...], (((1,), (1,)), ((), ())), preferred_element_type=F32).astype(BF16)
+    pbfull[f] = jnp.broadcast_to(pb_ref[...].astype(F32)[None, :], (8, cols))
     pl.semaphore_wait(barrier, n_dp + n_f - 2)
 
     x_cp = []
@@ -111,22 +121,23 @@
 
     x = xrecv[...].reshape(slots, 128)
     length = x[:, samp : samp + 1]
-    first = []
+    first, p_cp = [], []
     for t in range(2 * frames + 1):
         xt = x if t == 0 else pltpu.roll(x, 128 - 5 * t, axis=1)
         v = jnp.dot(xt.astype(BF16), w0p[...], preferred_element_type=F32)
         first.append(gelu(norm_rows(v, gain_ref[0:1], nbias_ref[0:1])).astype(BF16))
-
-    p_cp = []
-    for o in range(1, n_f):
-        q = (f + n_f - o) % n_f
-        part = wfull.at[q, pl.ds(mine, ch)]
-        copy(part, part, wz_s.at[o], wz_r.at[o], d, q).wait_recv()
-        for c in range(1, n_chip):
-            i = o * n_chip + c
-            p_cp.append(copy(part, part, wp_s.at[i], wp_r.at[i], other(c) * 2 + core, f))
-            p_cp[-1].start()
-
+        for o in range(1, n_f):
+            if t != (2 * frames + 1) * o // n_f:
+                continue
+            q = (f + n_f - o) % n_f
+            part = wfull.at[q, pl.ds(mine, ch)]
+            copy(part, part, wz_s.at[o], wz_r.at[o], d, q).wait_recv()
+            for c in range(1, n_chip):
+                i = o * n_chip + c
+                p_cp.append(copy(part, part, wp_s.at[i], wp_r.at[i], other(c) * 2 + core, f))
+                p_cp[-1].start()
+
+    w1_cp.wait()
     normed, masked, masks = [], [], []
     for j in range(frames):
         taps = jnp.concatenate(first[2 * j : 2 * j + 3], axis=1)
@@ -246,12 +257,12 @@
     for o in range(1, n_dp):
         copy(hsum, hall.at[o], k_s.at[o], k_r.at[o], (d + n_dp - o) % n_dp, f).wait_recv()
         hown = hown + hall[o]
-    gb_ref[...] = hown[0:1].astype(BF16)
+    gb_ref[...] = hown[0].astype(BF16)
     for c in range(n_chip):
         at = other(c) if c else chip
         part = gwbuf.at[pl.ds((1 - core) * half + at * ch, ch)]
         copy(part, part, e_s.at[c], e_r.at[c], mate, f).wait_recv()
-    gw_ref[...] = gwbuf[...]
+    gw_ref[...] = dot_t(gwbuf[...], eye).astype(BF16)
     for one in x_cp + z_cp + pb_cp + p_cp + m_cp + a_cp + h_cp + b_cp + c_cp + k_cp + d_cp + e_cp:
         one.wait_send()
 
@@ -268,22 +279,23 @@
     n_chip, half = n_dp // 2, depth // 2
     ch = half // n_chip
     total = slots * frames
-    data = jnp.concatenate(
-        [waveform, lengths[:, None].astype(BF16), destination.astype(BF16),
-         jnp.zeros((rows, 128 - samp - 2), BF16)], axis=1)
     vmem = pl.BlockSpec(memory_space=pltpu.VMEM)
+    hbm = pl.BlockSpec(memory_space=pltpu.HBM)
     dma = lambda n: pltpu.SemaphoreType.DMA((n,))
     nc = n_f * n_chip
     feats, gw, gb = pl.pallas_call(
         functools.partial(fused, samp, n_dp, n_f, cap, frames),
         out_shape=(
             jax.ShapeDtypeStruct((total, width), BF16),
-            jax.ShapeDtypeStruct((depth, cols), BF16),
-            jax.ShapeDtypeStruct((1, cols), BF16),
+            jax.ShapeDtypeStruct((cols, depth), BF16),
+            jax.ShapeDtypeStruct((cols,), BF16),
         ),
-        in_specs=[vmem] * 8,
+        in_specs=[vmem] * 4 + [hbm] + [vmem] * 5,
         out_specs=(vmem,) * 3,
         scratch_shapes=[
+            pltpu.VMEM(conv1_weight.shape, BF16),
+            pltpu.SemaphoreType.DMA,
+            pltpu.VMEM((rows, 128), BF16),
             pltpu.VMEM((n_dp, cap, 128), F32),
             pltpu.VMEM((n_dp, cap, 128), F32),
             pltpu.VMEM((128, depth), BF16),
@@ -316,9 +328,9 @@
         cost_estimate=pl.CostEstimate(
             flops=2 * total * depth * (3 * depth + 2 * width),
             bytes_accessed=8 * depth * width, transcendentals=13 * slots * depth),
-    )(data, conv0_weight, conv1_weight, norm_gain, norm_bias, proj_weight,
-      proj_bias[None, :], cotangent.reshape(total, width))
-    return feats.reshape(slots, frames, width), gw, gb[0]
+    )(waveform, destination, lengths[None, :], conv0_weight, conv1_weight,
+      norm_gain, norm_bias, proj_weight.T, proj_bias, cotangent.reshape(total, width))
+    return feats.reshape(slots, frames, width), gw.T, gb
 
 
 def layer_norm(values, gain_vec, bias_vec):

time: 49.6 us -> 48.2 us (0.972)
  other arithmetic: 2.76 us -> 0 us
  Pallas kernels: 39.9 us -> 40.9 us
    reshape x1, local copies, waits for them, and re-layouts: 0.22 us -> 1.69 us  [local_fused(): cotangent.reshape(total, width)]
    convert_element_type x2 -> x0, other arithmetic: 1.4 us -> none  [the longest x1 0.74 us: local_fused(): destination.astype(BF16)]
    pallas_call x1, Pallas kernels: 39.9 us -> 40.9 us  [local_fused(): pl.pallas_call(functools.partial(fused, samp, n_dp, n_f, cap, frames), ou...]
    concatenate x1 -> x0, other arithmetic: 0.78 us -> none  [local_fused(): jnp.concatenate([waveform, lengths[:, None].astype(BF16), destination.ast...]
    broadcast_in_dim x2 -> x0, local copies, waits for them, and re-layouts: 0.68 us -> none  [the longest x1 0.68 us: local_fused(): proj_bias[None, :]]
    pallas_call x1 -> x0, other arithmetic: 0.58 us -> none  [local_fused(): pl.pallas_call(functools.partial(fused, samp, n_dp, n_f, cap, frames), ou...]
    unnamed x12 -> x19, local copies, waits for them, and re-layouts: 3.64 us -> 3.56 us
where the time goes in v2:
time: 48.2 us; the launch traced here: 48.1 us
  Pallas kernels  40.9 us (85%)
  local copies, waits for them, and re-layouts  6.41 us (13%)
  between operations  0.77 us (2%)
    pallas_call x1, Pallas kernels, local_fused(): pl.pallas_call(functools.partial(fused, samp, n_dp, n_f, cap, frames), ou...  40.9 us
    unnamed x19, local copies, waits for them, and re-layouts  3.56 us
    reshape x1, local copies, waits for them, and re-layouts, local_fused(): cotangent.reshape(total, width)  1.69 us
    reshape x1, local copies, waits for them, and re-layouts, local_fused(): return (feats.reshape(slots, frames, width), gw.T, gb)  1.17 us

profile of v2, /device:TPU:1, one launch (start us, length us, event | category | flops | bytes accessed | tf_op | source)
XLA Modules:
  0.0 48.1 jit_solution(10085342339449630706)
XLA Ops:
  0.6 0.0 copy-start.6
  0.6 0.0 copy-start.1
  0.7 0.0 copy-start.5
  0.7 0.0 copy-start.4
  0.7 0.0 copy-start.2
  0.7 0.0 copy-start.7
  0.7 0.0 copy-start.3
  0.7 0.8 %copy.13.dest_ref = s32[32,1]{1,0:T(8,128)S(1)} copy(s32[32,1]{0,1:T(1,128)} %param.11) | data formatting | bytes 256 | tf_op args[1]
  1.5 1.7 %reshape.12.cot_ref = bf16[256,1920]{1,0:T(8,128)(2,1)S(1)} reshape(bf16[64,4,1920]{2,1,0:T(4,128)(2,1)} %param.19) | data formatting | bytes 1966080 | tf_op jit(solution)/shard_map/reshape | solution.py:332
  3.2 0.0 copy-done.6
  3.2 0.0 copy-done.1
  3.2 0.0 copy-done.5
  3.2 0.0 copy-done.4
  3.2 0.0 copy-done.2
  3.2 0.0 copy-done.7
  3.2 0.0 copy-done.3
  3.2 0.0 copy-start
  3.3 1.4 %copy-done = bf16[1536,512]{1,0:T(8,128)(2,1)S(1)} copy-done((bf16[1536,512]{1,0:T(8,128)(2,1)S(1)}, bf16[1536,512]{1,0:T(8,128)(2,1)}, u32[]{:S(2)}) %copy-start) | copy-done | bytes 1572888
  4.7 40.9 %shard_map.121 = (bf16[256,1920]{1,0:T(8,128)(2,1)S(1)}, bf16[480,512]{1,0:T(8,128)(2,1)S(1)}, bf16[480]{0:T(512)(128)(2,1)S(1)}) custom-call(bf16[32,50]{1,0:T(8,128)(2,1)S(1)} %copy-done.3, s32[32,1]{1,0:T(8,128)S(1)} %copy.13.dest_ref, s32[1,32]{1,0:T(1,128)S(1)} %bitcast.5, bf16[10,512]{1,0:T(8,128)(2,1)S(1)} %copy-done.2, ...), custom_call_target="tpu_custom_call" | custom-call | flops 1409286144 | bytes 7864320 | tf_op jit(solution)/shard_map/pallas_call | solution.py:286
  45.5 1.2 %reshape.13 = bf16[64,4,1920]{2,1,0:T(4,128)(2,1)} reshape(bf16[256,1920]{1,0:T(8,128)(2,1)S(1)} %get-tuple-element.6) | data formatting | bytes 1966080 | tf_op jit(solution)/shard_map/reshape | solution.py:333
  46.7 0.8 %copy.16 = bf16[512,480]{0,1:T(8,128)(2,1)} copy(bf16[512,480]{0,1:T(8,128)(2,1)S(1)} %bitcast.3) | data formatting | bytes 983040
  47.5 0.6 %copy.17 = bf16[480]{0:T(512)(128)(2,1)} copy(bf16[480]{0:T(512)(128)(2,1)S(1)} %get-tuple-element.14) | data formatting | bytes 1920
Async XLA Ops:
  0.6 2.5 %copy-start.6 = (bf16[480]{0:T(512)(128)(2,1)S(1)}, bf16[480]{0:T(512)(128)(2,1)}, u32[]{:S(2)}) copy-start(bf16[480]{0:T(512)(128)(2,1)} %pb_ref.1) | copy-start | bytes 2884
  0.6 2.5 %copy-start.1 = (bf16[512,480]{0,1:T(8,128)(2,1)S(1)}, bf16[512,480]{0,1:T(8,128)(2,1)}, u32[]{:S(2)}) copy-start(bf16[512,480]{0,1:T(8,128)(2,1)} %param.17) | copy-start | bytes 1474564
  0.7 2.5 %copy-start.5 = (f32[3,512]{1,0:T(4,128)S(1)}, f32[3,512]{1,0:T(4,128)}, u32[]{:S(2)}) copy-start(f32[3,512]{1,0:T(4,128)} %nbias_ref.1) | copy-start | bytes 18436
  0.7 2.5 %copy-start.4 = (f32[3,512]{1,0:T(4,128)S(1)}, f32[3,512]{1,0:T(4,128)}, u32[]{:S(2)}) copy-start(f32[3,512]{1,0:T(4,128)} %gain_ref.1) | copy-start | bytes 18436
  0.7 2.5 %copy-start.2 = (bf16[10,512]{1,0:T(8,128)(2,1)S(1)}, bf16[10,512]{1,0:T(8,128)(2,1)}, u32[]{:S(2)}) copy-start(bf16[10,512]{1,0:T(8,128)(2,1)} %w0_ref.1) | copy-start | bytes 30724
  0.7 2.5 %copy-start.7 = (s32[32]{0:T(128)S(1)}, s32[32]{0:T(128)}, u32[]{:S(2)}) copy-start(s32[32]{0:T(128)} %param.12) | copy-start | bytes 388
  0.7 2.5 %copy-start.3 = (bf16[32,50]{1,0:T(8,128)(2,1)S(1)}, bf16[32,50]{1,0:T(8,128)(2,1)}, u32[]{:S(2)}) copy-start(bf16[32,50]{1,0:T(8,128)(2,1)} %wave_ref.1) | copy-start | bytes 9604
  3.2 1.4 %copy-start = (bf16[1536,512]{1,0:T(8,128)(2,1)S(1)}, bf16[1536,512]{1,0:T(8,128)(2,1)}, u32[]{:S(2)}) copy-start(bf16[1536,512]{1,0:T(8,128)(2,1)} %w1_hbm.1) | copy-start | bytes 4718596

commit v3 on v2

--- a/solution.py
+++ b/solution.py
@@ -30,9 +30,9 @@
 
 def fused(
     samp, n_dp, n_f, cap, frames,
-    wave_ref, dest_ref, len_ref, w0_ref, w1_hbm, gain_ref, nbias_ref, pw_ref, pb_ref, cot_ref,
-    feat_ref, gw_ref, gb_ref,
-    w1_ref, w1_sem, table_ref, xsend, xrecv, w0p, wfull, pbfull, cotb, normed_ref, masked_ref, mask_ref,
+    wave_ref, dest_ref, len_ref, w0_ref, w1_hbm, gain_ref, nbias_ref, pw_hbm, pb_ref, cot_hbm,
+    feat_hbm, gw_ref, gb_ref,
+    w1_ref, pw_ref, cot_ref, feat_ref, l_sem, b2send, table_ref, xsend, xrecv, w0p, wfull, pbfull, cotb, normed_ref, masked_ref, mask_ref,
     asend, arecv, gown, bsend, brecv, csend, crecv, gwbuf,
     hsend, hrecv, hsum, hall,
     x_s, x_r, wz_s, wz_r, wp_s, wp_r, wm_s, wm_r, pb_s, pb_r,
@@ -45,11 +45,15 @@
     cx = chip % 2
     cy = chip // 2
     n_chip = n_dp // 2
-    cols, depth = pw_ref.shape
+    cols, depth = pw_hbm.shape
     half = depth // 2
     ch = half // n_chip
     slots = n_dp * cap
     mate = chip * 2 + (1 - core)
+    along_x = cy * 2 + (1 - cx)
+    along_y = (1 - cy) * 2 + cx
+    near = along_x * (1 - core) + along_y * core
+    far = along_y * (1 - core) + along_x * core
 
     def other(c):
         return ((cy + c // 2) % 2) * 2 + (cx + c % 2) % 2
@@ -60,8 +64,11 @@
             device_id=(dd, ff), device_id_type=MESH,
         )
 
-    w1_cp = pltpu.make_async_copy(w1_hbm, w1_ref, w1_sem)
-    w1_cp.start()
+    pw_cp = pltpu.make_async_copy(pw_hbm, pw_ref, l_sem.at[0])
+    cot_cp = pltpu.make_async_copy(cot_hbm, cot_ref, l_sem.at[1])
+    w1_cp = pltpu.make_async_copy(w1_hbm, w1_ref, l_sem.at[2])
+    for one in (pw_cp, cot_cp, w1_cp):
+        one.start()
     barrier = pltpu.get_barrier_semaphore()
     for o in range(1, n_dp):
         pl.semaphore_signal(barrier, inc=1, device_id=((d + o) % n_dp, f), device_id_type=MESH)
@@ -78,7 +85,8 @@
     table_ref[:, 0:samp] = wave_ref[...]
     table = table_ref[...]
     lane = lane.astype(F32)
-    target = dest_ref[...].astype(F32)
+    named_row = jnp.broadcast_to(dest_ref[...].astype(F32), (rows, rows))
+    target = jnp.sum(jnp.where(tri_r == tri_c, named_row, 0.0), axis=1, keepdims=True)
     named = (target == lane).astype(F32)
     earlier = (tri_c < tri_r).astype(F32).astype(BF16)
     before = jnp.dot(earlier, named.astype(BF16), preferred_element_type=F32)
@@ -90,6 +98,7 @@
     eye_r = lax.broadcasted_iota(jnp.int32, (depth, depth), 0)
     eye_c = lax.broadcasted_iota(jnp.int32, (depth, depth), 1)
     eye = (eye_r == eye_c).astype(F32).astype(BF16)
+    pw_cp.wait()
     wfull[f] = lax.dot_general(
         eye, pw_ref[...], (((1,), (1,)), ((), ())), preferred_element_type=F32).astype(BF16)
     pbfull[f] = jnp.broadcast_to(pb_ref[...].astype(F32)[None, :], (8, cols))
@@ -113,6 +122,7 @@
     xrecv[d] = xsend[d]
     w0p[...] = jnp.zeros_like(w0p)
     w0p[0 : w0_ref.shape[0], :] = w0_ref[...]
+    cot_cp.wait()
     for b in range(n_f):
         cotb[b] = cot_ref[:, b * cols : (b + 1) * cols]
     for o in range(1, n_dp):
@@ -184,12 +194,11 @@
         both = gown[o] + arecv[o].astype(F32)
         gown[o] = both
         bsend[o] = both.astype(BF16)
-        for c in range(1, n_chip):
-            to = other(c)
+        for c, to in ((2, 3 - chip), (1, near)):
             i = o * n_chip + c
             b_cp.append(copy(
                 bsend.at[o, pl.ds(to * ch, ch)], brecv.at[i],
-                b_s.at[i], b_r.at[i], to * 2 + core, f))
+                b_s.at[i], b_r.at[i], near * 2 + core, f))
             b_cp[-1].start()
 
     m_cp = []
@@ -204,21 +213,31 @@
         m_cp.append(copy(block, block, wm_s.at[o], wm_r.at[o], mate, f))
         m_cp[-1].start()
         copy(pbfull.at[q], pbfull.at[q], pb_s.at[o], pb_r.at[o], d, q).wait_recv()
+    for o in order:
+        i = o * n_chip
+        copy(brecv.at[i + 2], brecv.at[i + 2], b_s.at[i + 2], b_r.at[i + 2], near * 2 + core, f).wait_recv()
+        b2send[o] = (gown[o, pl.ds(far * ch, ch), :] + brecv[i + 2].astype(F32)).astype(BF16)
+        b_cp.append(copy(
+            b2send.at[o], brecv.at[i + 3], b_s.at[i + 3], b_r.at[i + 3], far * 2 + core, f))
+        b_cp[-1].start()
     for o in range(1, n_f):
         q = (f + n_f - o) % n_f
         block = wfull.at[q, pl.ds((1 - core) * half, half)]
         copy(block, block, wm_s.at[o], wm_r.at[o], mate, f).wait_recv()
-    for b in range(n_f):
+    def project(b):
         v = jnp.dot(normed_ref[...], wfull[b], preferred_element_type=F32) + pbfull[b][0:1]
         feat_ref[:, b * cols : (b + 1) * cols] = (v * mask_ref[:, 0:1]).astype(BF16)
 
+    for b in range(n_f // 2):
+        project(b)
+
     c_cp = []
     own = None
     for o in order:
         part = gown[o, pl.ds(chip * ch, ch), :]
-        for c in range(1, n_chip):
+        for c, to in ((1, near), (3, far)):
             i = o * n_chip + c
-            copy(brecv.at[i], brecv.at[i], b_s.at[i], b_r.at[i], other(c) * 2 + core, f).wait_recv()
+            copy(brecv.at[i], brecv.at[i], b_s.at[i], b_r.at[i], to * 2 + core, f).wait_recv()
             part = part + brecv[i].astype(F32)
         if o:
             csend[o] = part.astype(BF16)
@@ -226,6 +245,10 @@
             c_cp[-1].start()
         else:
             own = part
+    for b in range(n_f // 2, n_f):
+        project(b)
+    feat_cp = pltpu.make_async_copy(feat_ref, feat_hbm, l_sem.at[3])
+    feat_cp.start()
     hown = hsend[0]
     for o in range(1, n_f):
         q = (f + n_f - o) % n_f
@@ -263,6 +286,7 @@
         part = gwbuf.at[pl.ds((1 - core) * half + at * ch, ch)]
         copy(part, part, e_s.at[c], e_r.at[c], mate, f).wait_recv()
     gw_ref[...] = dot_t(gwbuf[...], eye).astype(BF16)
+    feat_cp.wait()
     for one in x_cp + z_cp + pb_cp + p_cp + m_cp + a_cp + h_cp + b_cp + c_cp + k_cp + d_cp + e_cp:
         one.wait_send()
 
@@ -290,11 +314,15 @@
             jax.ShapeDtypeStruct((cols, depth), BF16),
             jax.ShapeDtypeStruct((cols,), BF16),
         ),
-        in_specs=[vmem] * 4 + [hbm] + [vmem] * 5,
-        out_specs=(vmem,) * 3,
+        in_specs=[vmem] * 4 + [hbm] + [vmem] * 2 + [hbm, vmem, hbm],
+        out_specs=(hbm, vmem, vmem),
         scratch_shapes=[
             pltpu.VMEM(conv1_weight.shape, BF16),
-            pltpu.SemaphoreType.DMA,
+            pltpu.VMEM((cols, depth), BF16),
+            pltpu.VMEM((total, width), BF16),
+            pltpu.VMEM((total, width), BF16),
+            dma(4),
+            pltpu.VMEM((n_f, ch, cols), BF16),
             pltpu.VMEM((rows, 128), BF16),
             pltpu.VMEM((n_dp, cap, 128), F32),
             pltpu.VMEM((n_dp, cap, 128), F32),
@@ -324,11 +352,11 @@
             dma(n_f), dma(n_f), dma(n_dp), dma(n_dp),
         ],
         compiler_params=pltpu.CompilerParams(
-            collective_id=0, has_side_effects=True, vmem_limit_bytes=48 * 1024 * 1024),
+            collective_id=0, has_side_effects=True, vmem_limit_bytes=60 * 1024 * 1024),
         cost_estimate=pl.CostEstimate(
             flops=2 * total * depth * (3 * depth + 2 * width),
             bytes_accessed=8 * depth * width, transcendentals=13 * slots * depth),
-    )(waveform, destination, lengths[None, :], conv0_weight, conv1_weight,
+    )(waveform, destination.reshape(1, -1), lengths[None, :], conv0_weight, conv1_weight,
       norm_gain, norm_bias, proj_weight.T, proj_bias, cotangent.reshape(total, width))
     return feats.reshape(slots, frames, width), gw.T, gb
 

time: 48.2 us -> 49.9 us (1.035)
  Pallas kernels: 40.9 us -> 42.6 us
    unnamed x19 -> x6, local copies, waits for them, and re-layouts: 3.56 us -> 1.35 us
    pallas_call x1, Pallas kernels: 40.9 us -> 42.6 us  [local_fused(): pl.pallas_call(functools.partial(fused, samp, n_dp, n_f, cap, frames), ou...]
    reshape x1, local copies, waits for them, and re-layouts: 1.17 us -> 2.64 us  [local_fused(): return (feats.reshape(slots, frames, width), gw.T, gb)]
    reshape x1, local copies, waits for them, and re-layouts: 1.69 us -> 2.44 us  [local_fused(): cotangent.reshape(total, width)]
where the time goes in v3:
time: 49.9 us; the launch traced here: 49.7 us
  Pallas kernels  42.6 us (85%)
  local copies, waits for them, and re-layouts  6.44 us (13%)
  between operations  0.66 us (1%)
    pallas_call x1, Pallas kernels, local_fused(): pl.pallas_call(functools.partial(fused, samp, n_dp, n_f, cap, frames), ou...  42.6 us
    reshape x1, local copies, waits for them, and re-layouts, local_fused(): return (feats.reshape(slots, frames, width), gw.T, gb)  2.64 us
    reshape x1, local copies, waits for them, and re-layouts, local_fused(): cotangent.reshape(total, width)  2.44 us
    unnamed x6, local copies, waits for them, and re-layouts  1.35 us

profile of v3, /device:TPU:1, one launch (start us, length us, event | category | flops | bytes accessed | tf_op | source)
XLA Modules:
  0.0 49.7 jit_solution(4458075956578189786)
XLA Ops:
  0.6 2.4 %reshape.16.cot_hbm = bf16[256,1920]{1,0:T(8,128)(2,1)} reshape(bf16[64,4,1920]{2,1,0:T(4,128)(2,1)} %param.19) | data formatting | bytes 1966080 | tf_op jit(solution)/shard_map/reshape | solution.py:360
  3.1 42.6 %shard_map.121 = (bf16[256,1920]{1,0:T(8,128)(2,1)}, bf16[480,512]{1,0:T(8,128)(2,1)}, bf16[480]{0:T(512)(128)(2,1)}) custom-call(bf16[32,50]{1,0:T(8,128)(2,1)} %wave_ref.1, s32[1,32]{1,0:T(1,128)} %bitcast.6, s32[1,32]{1,0:T(1,128)} %bitcast.7, bf16[10,512]{1,0:T(8,128)(2,1)} %w0_ref.1, bf16[1536,512]{1,0:T(8,128)(2,1)} %w1_hbm.1, f32[3,512]{1,0:T(4,128)} %gain_ref.1, ...), custom_call_target="tpu_custom_call" | custom-call | flops 1409286144 | bytes 7864320 | tf_op jit(solution)/shard_map/pallas_call | solution.py:310
  45.7 0.0 copy-start
  45.7 0.0 copy-start.1
  45.7 2.6 %reshape.17 = bf16[64,4,1920]{2,1,0:T(4,128)(2,1)} reshape(bf16[256,1920]{1,0:T(8,128)(2,1)} %get-tuple-element.6) | data formatting | bytes 1966080 | tf_op jit(solution)/shard_map/reshape | solution.py:361
  48.3 0.0 copy-done
  48.3 0.8 %copy.15 = bf16[512,480]{0,1:T(8,128)(2,1)} copy(bf16[512,480]{0,1:T(8,128)(2,1)S(1)} %bitcast.4) | data formatting | bytes 983040
  49.1 0.0 copy-done.1
  49.1 0.6 %copy.16 = bf16[480]{0:T(512)(128)(2,1)} copy(bf16[480]{0:T(512)(128)(2,1)S(1)} %copy-done.1) | data formatting | bytes 1920
Async XLA Ops:
  45.7 2.7 %copy-start = (bf16[480,512]{1,0:T(8,128)(2,1)S(1)}, bf16[480,512]{1,0:T(8,128)(2,1)}, u32[]{:S(2)}) copy-start(bf16[480,512]{1,0:T(8,128)(2,1)} %get-tuple-element.7) | copy-start | bytes 1474564
  45.7 3.4 %copy-start.1 = (bf16[480]{0:T(512)(128)(2,1)S(1)}, bf16[480]{0:T(512)(128)(2,1)}, u32[]{:S(2)}) copy-start(bf16[480]{0:T(512)(128)(2,1)} %get-tuple-element.14) | copy-start | bytes 2884

commit v4 on v2

--- a/solution.py
+++ b/solution.py
@@ -32,7 +32,7 @@
     samp, n_dp, n_f, cap, frames,
     wave_ref, dest_ref, len_ref, w0_ref, w1_hbm, gain_ref, nbias_ref, pw_ref, pb_ref, cot_ref,
     feat_ref, gw_ref, gb_ref,
-    w1_ref, w1_sem, table_ref, xsend, xrecv, w0p, wfull, pbfull, cotb, normed_ref, masked_ref, mask_ref,
+    w1_ref, w1_sem, perm_ref, table_ref, xsend, xrecv, w0p, wfull, pbfull, cotb, normed_ref, masked_ref, mask_ref,
     asend, arecv, gown, bsend, brecv, csend, crecv, gwbuf,
     hsend, hrecv, hsum, hall,
     x_s, x_r, wz_s, wz_r, wp_s, wp_r, wm_s, wm_r, pb_s, pb_r,
@@ -78,7 +78,8 @@
     table_ref[:, 0:samp] = wave_ref[...]
     table = table_ref[...]
     lane = lane.astype(F32)
-    target = dest_ref[...].astype(F32)
+    named_row = jnp.broadcast_to(dest_ref[...].astype(F32), (rows, rows))
+    target = jnp.sum(jnp.where(tri_r == tri_c, named_row, 0.0), axis=1, keepdims=True)
     named = (target == lane).astype(F32)
     earlier = (tri_c < tri_r).astype(F32).astype(BF16)
     before = jnp.dot(earlier, named.astype(BF16), preferred_element_type=F32)
@@ -87,19 +88,19 @@
     placing = (place == lane).astype(F32).astype(BF16)
     placed = dot_t(placing, table)[:slots]
     xsend[...] = placed.reshape(n_dp, cap, 128)
+    pl.semaphore_wait(barrier, n_dp + n_f - 2)
+
+    x_cp = []
+    for o in range(1, n_dp):
+        p = (d + o) % n_dp
+        x_cp.append(copy(xsend.at[p], xrecv.at[d], x_s.at[o], x_r.at[o], p, f))
+        x_cp[-1].start()
     eye_r = lax.broadcasted_iota(jnp.int32, (depth, depth), 0)
     eye_c = lax.broadcasted_iota(jnp.int32, (depth, depth), 1)
     eye = (eye_r == eye_c).astype(F32).astype(BF16)
     wfull[f] = lax.dot_general(
         eye, pw_ref[...], (((1,), (1,)), ((), ())), preferred_element_type=F32).astype(BF16)
     pbfull[f] = jnp.broadcast_to(pb_ref[...].astype(F32)[None, :], (8, cols))
-    pl.semaphore_wait(barrier, n_dp + n_f - 2)
-
-    x_cp = []
-    for o in range(1, n_dp):
-        p = (d + o) % n_dp
-        x_cp.append(copy(xsend.at[p], xrecv.at[d], x_s.at[o], x_r.at[o], p, f))
-        x_cp[-1].start()
     mine = core * half + chip * ch
     z_cp, pb_cp = [], []
     for o in range(1, n_f):
@@ -113,6 +114,13 @@
     xrecv[d] = xsend[d]
     w0p[...] = jnp.zeros_like(w0p)
     w0p[0 : w0_ref.shape[0], :] = w0_ref[...]
+    total = slots * frames
+    pr = lax.broadcasted_iota(jnp.int32, (total, total), 0)
+    pc = lax.broadcasted_iota(jnp.int32, (total, total), 1) * frames
+    hit = pr == pc
+    for j in range(1, frames):
+        hit = hit | (pr == pc - j * (total - 1))
+    perm_ref[...] = hit.astype(F32).astype(BF16)
     for b in range(n_f):
         cotb[b] = cot_ref[:, b * cols : (b + 1) * cols]
     for o in range(1, n_dp):
@@ -147,12 +155,8 @@
         mj = (length >= 10.0 * j + 20.0).astype(F32)
         normed.append(nj)
         masks.append(jnp.broadcast_to(mj, (slots, 128)).astype(BF16))
-    total = slots * frames
-    pr = lax.broadcasted_iota(jnp.int32, (total, total), 0)
-    pc = lax.broadcasted_iota(jnp.int32, (total, total), 1)
-    perm = ((pr % frames) * slots + pr // frames == pc).astype(F32).astype(BF16)
-    nrm = jnp.dot(perm, jnp.concatenate(normed, axis=0), preferred_element_type=F32)
-    msk = jnp.dot(perm, jnp.concatenate(masks, axis=0), preferred_element_type=F32)
+    nrm = jnp.dot(perm_ref[...], jnp.concatenate(normed, axis=0), preferred_element_type=F32)
+    msk = jnp.dot(perm_ref[...], jnp.concatenate(masks, axis=0), preferred_element_type=F32)
     normed_ref[...] = nrm.astype(BF16)
     masked_ref[...] = (nrm * msk[:, 0:1]).astype(BF16)
     mask_ref[...] = msk
@@ -169,15 +173,6 @@
     for o in order:
         b = (f + o) % n_f
         gown[o] = dot_t(ours, cotb[b])
-    h_cp = []
-    ones = mask_ref[...].astype(BF16)
-    for o in order:
-        b = (f + o) % n_f
-        hsend[o] = dot_t(ones, cotb[b])[0:8]
-        if o:
-            h_cp.append(copy(hsend.at[o], hrecv.at[o], h_s.at[o], h_r.at[o], d, b))
-            h_cp[-1].start()
-
     b_cp = []
     for o in order:
         copy(asend.at[o], arecv.at[o], a_s.at[o], a_r.at[o], mate, f).wait_recv()
@@ -192,6 +187,15 @@
                 b_s.at[i], b_r.at[i], to * 2 + core, f))
             b_cp[-1].start()
 
+    h_cp = []
+    ones = mask_ref[...].astype(BF16)
+    for o in order:
+        b = (f + o) % n_f
+        hsend[o] = dot_t(ones, cotb[b])[0:8]
+        if o:
+            h_cp.append(copy(hsend.at[o], hrecv.at[o], h_s.at[o], h_r.at[o], d, b))
+            h_cp[-1].start()
+
     m_cp = []
     for o in range(1, n_f):
         q = (f + n_f - o) % n_f
@@ -208,9 +212,12 @@
         q = (f + n_f - o) % n_f
         block = wfull.at[q, pl.ds((1 - core) * half, half)]
         copy(block, block, wm_s.at[o], wm_r.at[o], mate, f).wait_recv()
-    for b in range(n_f):
+    def project(b):
         v = jnp.dot(normed_ref[...], wfull[b], preferred_element_type=F32) + pbfull[b][0:1]
         feat_ref[:, b * cols : (b + 1) * cols] = (v * mask_ref[:, 0:1]).astype(BF16)
+
+    for b in range(n_f // 2):
+        project(b)
 
     c_cp = []
     own = None
@@ -226,6 +233,8 @@
             c_cp[-1].start()
         else:
             own = part
+    for b in range(n_f // 2, n_f):
+        project(b)
     hown = hsend[0]
     for o in range(1, n_f):
         q = (f + n_f - o) % n_f
@@ -295,6 +304,7 @@
         scratch_shapes=[
             pltpu.VMEM(conv1_weight.shape, BF16),
             pltpu.SemaphoreType.DMA,
+            pltpu.VMEM((total, total), BF16),
             pltpu.VMEM((rows, 128), BF16),
             pltpu.VMEM((n_dp, cap, 128), F32),
             pltpu.VMEM((n_dp, cap, 128), F32),
@@ -328,7 +338,7 @@
         cost_estimate=pl.CostEstimate(
             flops=2 * total * depth * (3 * depth + 2 * width),
             bytes_accessed=8 * depth * width, transcendentals=13 * slots * depth),
-    )(waveform, destination, lengths[None, :], conv0_weight, conv1_weight,
+    )(waveform, destination.reshape(1, -1), lengths[None, :], conv0_weight, conv1_weight,
       norm_gain, norm_bias, proj_weight.T, proj_bias, cotangent.reshape(total, width))
     return feats.reshape(slots, frames, width), gw.T, gb
 

time: 48.2 us -> 48.7 us (1.010)
  Pallas kernels: 40.9 us -> 42 us
  local copies, waits for them, and re-layouts: 6.41 us -> 5.68 us
    pallas_call x1, Pallas kernels: 40.9 us -> 42 us  [local_fused(): pl.pallas_call(functools.partial(fused, samp, n_dp, n_f, cap, frames), ou...]
    unnamed x19 -> x20, local copies, waits for them, and re-layouts: 3.56 us -> 2.78 us
where the time goes in v4:
time: 48.7 us; the launch traced here: 48.5 us
  Pallas kernels  42 us (86%)
  local copies, waits for them, and re-layouts  5.68 us (12%)
  between operations  0.79 us (2%)
    pallas_call x1, Pallas kernels, local_fused(): pl.pallas_call(functools.partial(fused, samp, n_dp, n_f, cap, frames), ou...  42 us
    unnamed x20, local copies, waits for them, and re-layouts  2.78 us
    reshape x1, local copies, waits for them, and re-layouts, local_fused(): cotangent.reshape(total, width)  1.74 us
    reshape x1, local copies, waits for them, and re-layouts, local_fused(): return (feats.reshape(slots, frames, width), gw.T, gb)  1.17 us

profile of v4, /device:TPU:1, one launch (start us, length us, event | category | flops | bytes accessed | tf_op | source)
XLA Modules:
  0.0 48.5 jit_solution(1297879662195273475)
XLA Ops:
  0.6 0.0 copy-start.6
  0.6 0.0 copy-start.1
  0.7 0.0 copy-start.5
  0.7 0.0 copy-start.4
  0.7 0.0 copy-start.2
  0.7 0.0 copy-start.8
  0.7 0.0 copy-start.7
  0.7 0.0 copy-start.3
  0.7 1.7 %reshape.16.cot_ref = bf16[256,1920]{1,0:T(8,128)(2,1)S(1)} reshape(bf16[64,4,1920]{2,1,0:T(4,128)(2,1)} %param.19) | data formatting | bytes 1966080 | tf_op jit(solution)/shard_map/reshape | solution.py:342
  2.5 0.0 copy-done.6
  2.5 0.0 copy-done.1
  2.5 0.0 copy-done.5
  2.5 0.0 copy-done.4
  2.5 0.0 copy-done.2
  2.5 0.0 copy-done.8
  2.5 0.0 copy-done.7
  2.5 0.0 copy-done.3
  2.5 0.0 copy-start
  2.5 1.4 %copy-done = bf16[1536,512]{1,0:T(8,128)(2,1)S(1)} copy-done((bf16[1536,512]{1,0:T(8,128)(2,1)S(1)}, bf16[1536,512]{1,0:T(8,128)(2,1)}, u32[]{:S(2)}) %copy-start) | copy-done | bytes 1572888
  3.9 42.0 %shard_map.121 = (bf16[256,1920]{1,0:T(8,128)(2,1)S(1)}, bf16[480,512]{1,0:T(8,128)(2,1)S(1)}, bf16[480]{0:T(512)(128)(2,1)S(1)}) custom-call(bf16[32,50]{1,0:T(8,128)(2,1)S(1)} %copy-done.3, s32[1,32]{1,0:T(1,128)S(1)} %bitcast.6, s32[1,32]{1,0:T(1,128)S(1)} %bitcast.7, bf16[10,512]{1,0:T(8,128)(2,1)S(1)} %copy-done.2, bf16[1536,512]{1,0:T(8,128)(2,1)S(1)} %copy-done, ...), custom_call_target="tpu_custom_call" | custom-call | flops 1409286144 | bytes 7864320 | tf_op jit(solution)/shard_map/pallas_call | solution.py:295
  46.0 1.2 %reshape.17 = bf16[64,4,1920]{2,1,0:T(4,128)(2,1)} reshape(bf16[256,1920]{1,0:T(8,128)(2,1)S(1)} %get-tuple-element.6) | data formatting | bytes 1966080 | tf_op jit(solution)/shard_map/reshape | solution.py:343
  47.1 0.8 %copy.15 = bf16[512,480]{0,1:T(8,128)(2,1)} copy(bf16[512,480]{0,1:T(8,128)(2,1)S(1)} %bitcast.4) | data formatting | bytes 983040
  47.9 0.6 %copy.16 = bf16[480]{0:T(512)(128)(2,1)} copy(bf16[480]{0:T(512)(128)(2,1)S(1)} %get-tuple-element.14) | data formatting | bytes 1920
Async XLA Ops:
  0.6 1.8 %copy-start.6 = (bf16[480]{0:T(512)(128)(2,1)S(1)}, bf16[480]{0:T(512)(128)(2,1)}, u32[]{:S(2)}) copy-start(bf16[480]{0:T(512)(128)(2,1)} %pb_ref.1) | copy-start | bytes 2884
  0.6 1.8 %copy-start.1 = (bf16[512,480]{0,1:T(8,128)(2,1)S(1)}, bf16[512,480]{0,1:T(8,128)(2,1)}, u32[]{:S(2)}) copy-start(bf16[512,480]{0,1:T(8,128)(2,1)} %param.17) | copy-start | bytes 1474564
  0.7 1.8 %copy-start.5 = (f32[3,512]{1,0:T(4,128)S(1)}, f32[3,512]{1,0:T(4,128)}, u32[]{:S(2)}) copy-start(f32[3,512]{1,0:T(4,128)} %nbias_ref.1) | copy-start | bytes 18436
  0.7 1.8 %copy-start.4 = (f32[3,512]{1,0:T(4,128)S(1)}, f32[3,512]{1,0:T(4,128)}, u32[]{:S(2)}) copy-start(f32[3,512]{1,0:T(4,128)} %gain_ref.1) | copy-start | bytes 18436
  0.7 1.8 %copy-start.2 = (bf16[10,512]{1,0:T(8,128)(2,1)S(1)}, bf16[10,512]{1,0:T(8,128)(2,1)}, u32[]{:S(2)}) copy-start(bf16[10,512]{1,0:T(8,128)(2,1)} %w0_ref.1) | copy-start | bytes 30724
  0.7 1.8 %copy-start.8 = (s32[32]{0:T(128)S(1)}, s32[32]{0:T(128)}, u32[]{:S(2)}) copy-start(s32[32]{0:T(128)} %param.12) | copy-start | bytes 388
  0.7 1.8 %copy-start.7 = (s32[32,1]{0,1:T(1,128)S(1)}, s32[32,1]{0,1:T(1,128)}, u32[]{:S(2)}) copy-start(s32[32,1]{0,1:T(1,128)} %param.11) | copy-start | bytes 388
  0.7 1.8 %copy-start.3 = (bf16[32,50]{1,0:T(8,128)(2,1)S(1)}, bf16[32,50]{1,0:T(8,128)(2,1)}, u32[]{:S(2)}) copy-start(bf16[32,50]{1,0:T(8,128)(2,1)} %wave_ref.1) | copy-start | bytes 9604
  2.5 1.4 %copy-start = (bf16[1536,512]{1,0:T(8,128)(2,1)S(1)}, bf16[1536,512]{1,0:T(8,128)(2,1)}, u32[]{:S(2)}) copy-start(bf16[1536,512]{1,0:T(8,128)(2,1)} %w1_hbm.1) | copy-start | bytes 4718596

commit v5 on v4

--- a/solution.py
+++ b/solution.py
@@ -196,29 +196,6 @@
             h_cp.append(copy(hsend.at[o], hrecv.at[o], h_s.at[o], h_r.at[o], d, b))
             h_cp[-1].start()
 
-    m_cp = []
-    for o in range(1, n_f):
-        q = (f + n_f - o) % n_f
-        for c in range(1, n_chip):
-            i = o * n_chip + c
-            theirs_at = core * half + other(c) * ch
-            part = wfull.at[q, pl.ds(theirs_at, ch)]
-            copy(part, part, wp_s.at[i], wp_r.at[i], other(c) * 2 + core, f).wait_recv()
-        block = wfull.at[q, pl.ds(core * half, half)]
-        m_cp.append(copy(block, block, wm_s.at[o], wm_r.at[o], mate, f))
-        m_cp[-1].start()
-        copy(pbfull.at[q], pbfull.at[q], pb_s.at[o], pb_r.at[o], d, q).wait_recv()
-    for o in range(1, n_f):
-        q = (f + n_f - o) % n_f
-        block = wfull.at[q, pl.ds((1 - core) * half, half)]
-        copy(block, block, wm_s.at[o], wm_r.at[o], mate, f).wait_recv()
-    def project(b):
-        v = jnp.dot(normed_ref[...], wfull[b], preferred_element_type=F32) + pbfull[b][0:1]
-        feat_ref[:, b * cols : (b + 1) * cols] = (v * mask_ref[:, 0:1]).astype(BF16)
-
-    for b in range(n_f // 2):
-        project(b)
-
     c_cp = []
     own = None
     for o in order:
@@ -233,8 +210,18 @@
             c_cp[-1].start()
         else:
             own = part
-    for b in range(n_f // 2, n_f):
-        project(b)
+    m_cp = []
+    for o in range(1, n_f):
+        q = (f + n_f - o) % n_f
+        for c in range(1, n_chip):
+            i = o * n_chip + c
+            theirs_at = core * half + other(c) * ch
+            part = wfull.at[q, pl.ds(theirs_at, ch)]
+            copy(part, part, wp_s.at[i], wp_r.at[i], other(c) * 2 + core, f).wait_recv()
+        block = wfull.at[q, pl.ds(core * half, half)]
+        m_cp.append(copy(block, block, wm_s.at[o], wm_r.at[o], mate, f))
+        m_cp[-1].start()
+        copy(pbfull.at[q], pbfull.at[q], pb_s.at[o], pb_r.at[o], d, q).wait_recv()
     hown = hsend[0]
     for o in range(1, n_f):
         q = (f + n_f - o) % n_f
@@ -258,6 +245,17 @@
         d_cp[-1].start()
     e_cp = [copy(src, src, e_s.at[0], e_r.at[0], mate, f)]
     e_cp[0].start()
+    for o in range(1, n_f):
+        q = (f + n_f - o) % n_f
+        block = wfull.at[q, pl.ds((1 - core) * half, half)]
+        copy(block, block, wm_s.at[o], wm_r.at[o], mate, f).wait_recv()
+    def project(b):
+        v = jnp.dot(normed_ref[...], wfull[b], preferred_element_type=F32) + pbfull[b][0:1]
+        feat_ref[:, b * cols : (b + 1) * cols] = (v * mask_ref[:, 0:1]).astype(BF16)
+
+    for b in range(n_f):
+        project(b)
+
     for c in range(1, n_chip):
         part = gwbuf.at[pl.ds(core * half + other(c) * ch, ch)]
         copy(part, part, d_s.at[c], d_r.at[c], other(c) * 2 + core, f).wait_recv()

time: 48.7 us -> 48.2 us (0.990)
  no operation moved by 1% of the time
where the time goes in v5:
time: 48.2 us; the launch traced here: 48 us
  Pallas kernels  41.6 us (86%)
  local copies, waits for them, and re-layouts  5.68 us (12%)
  between operations  0.79 us (2%)
    pallas_call x1, Pallas kernels, local_fused(): pl.pallas_call(functools.partial(fused, samp, n_dp, n_f, cap, frames), ou...  41.6 us
    unnamed x20, local copies, waits for them, and re-layouts  2.78 us
    reshape x1, local copies, waits for them, and re-layouts, local_fused(): cotangent.reshape(total, width)  1.74 us
    reshape x1, local copies, waits for them, and re-layouts, local_fused(): return (feats.reshape(slots, frames, width), gw.T, gb)  1.17 us

profile of v5, /device:TPU:1, one launch (start us, length us, event | category | flops | bytes accessed | tf_op | source)
XLA Modules:
  0.0 48.0 jit_solution(1102232321814015793)
XLA Ops:
  0.6 0.0 copy-start.6
  0.6 0.0 copy-start.1
  0.7 0.0 copy-start.5
  0.7 0.0 copy-start.4
  0.7 0.0 copy-start.2
  0.7 0.0 copy-start.8
  0.7 0.0 copy-start.7
  0.7 0.0 copy-start.3
  0.7 1.7 %reshape.16.cot_ref = bf16[256,1920]{1,0:T(8,128)(2,1)S(1)} reshape(bf16[64,4,1920]{2,1,0:T(4,128)(2,1)} %param.19) | data formatting | bytes 1966080 | tf_op jit(solution)/shard_map/reshape | solution.py:340
  2.5 0.0 copy-done.6
  2.5 0.0 copy-done.1
  2.5 0.0 copy-done.5
  2.5 0.0 copy-done.4
  2.5 0.0 copy-done.2
  2.5 0.0 copy-done.8
  2.5 0.0 copy-done.7
  2.5 0.0 copy-done.3
  2.5 0.0 copy-start
  2.5 1.4 %copy-done = bf16[1536,512]{1,0:T(8,128)(2,1)S(1)} copy-done((bf16[1536,512]{1,0:T(8,128)(2,1)S(1)}, bf16[1536,512]{1,0:T(8,128)(2,1)}, u32[]{:S(2)}) %copy-start) | copy-done | bytes 1572888
  3.9 41.6 %shard_map.121 = (bf16[256,1920]{1,0:T(8,128)(2,1)S(1)}, bf16[480,512]{1,0:T(8,128)(2,1)S(1)}, bf16[480]{0:T(512)(128)(2,1)S(1)}) custom-call(bf16[32,50]{1,0:T(8,128)(2,1)S(1)} %copy-done.3, s32[1,32]{1,0:T(1,128)S(1)} %bitcast.6, s32[1,32]{1,0:T(1,128)S(1)} %bitcast.7, bf16[10,512]{1,0:T(8,128)(2,1)S(1)} %copy-done.2, bf16[1536,512]{1,0:T(8,128)(2,1)S(1)} %copy-done, ...), custom_call_target="tpu_custom_call" | custom-call | flops 1409286144 | bytes 7864320 | tf_op jit(solution)/shard_map/pallas_call | solution.py:293
  45.5 1.2 %reshape.17 = bf16[64,4,1920]{2,1,0:T(4,128)(2,1)} reshape(bf16[256,1920]{1,0:T(8,128)(2,1)S(1)} %get-tuple-element.6) | data formatting | bytes 1966080 | tf_op jit(solution)/shard_map/reshape | solution.py:341
  46.7 0.8 %copy.15 = bf16[512,480]{0,1:T(8,128)(2,1)} copy(bf16[512,480]{0,1:T(8,128)(2,1)S(1)} %bitcast.4) | data formatting | bytes 983040
  47.5 0.6 %copy.16 = bf16[480]{0:T(512)(128)(2,1)} copy(bf16[480]{0:T(512)(128)(2,1)S(1)} %get-tuple-element.14) | data formatting | bytes 1920
Async XLA Ops:
  0.6 1.8 %copy-start.6 = (bf16[480]{0:T(512)(128)(2,1)S(1)}, bf16[480]{0:T(512)(128)(2,1)}, u32[]{:S(2)}) copy-start(bf16[480]{0:T(512)(128)(2,1)} %pb_ref.1) | copy-start | bytes 2884
  0.6 1.8 %copy-start.1 = (bf16[512,480]{0,1:T(8,128)(2,1)S(1)}, bf16[512,480]{0,1:T(8,128)(2,1)}, u32[]{:S(2)}) copy-start(bf16[512,480]{0,1:T(8,128)(2,1)} %param.17) | copy-start | bytes 1474564
  0.7 1.8 %copy-start.5 = (f32[3,512]{1,0:T(4,128)S(1)}, f32[3,512]{1,0:T(4,128)}, u32[]{:S(2)}) copy-start(f32[3,512]{1,0:T(4,128)} %nbias_ref.1) | copy-start | bytes 18436
  0.7 1.8 %copy-start.4 = (f32[3,512]{1,0:T(4,128)S(1)}, f32[3,512]{1,0:T(4,128)}, u32[]{:S(2)}) copy-start(f32[3,512]{1,0:T(4,128)} %gain_ref.1) | copy-start | bytes 18436
  0.7 1.8 %copy-start.2 = (bf16[10,512]{1,0:T(8,128)(2,1)S(1)}, bf16[10,512]{1,0:T(8,128)(2,1)}, u32[]{:S(2)}) copy-start(bf16[10,512]{1,0:T(8,128)(2,1)} %w0_ref.1) | copy-start | bytes 30724
  0.7 1.8 %copy-start.8 = (s32[32]{0:T(128)S(1)}, s32[32]{0:T(128)}, u32[]{:S(2)}) copy-start(s32[32]{0:T(128)} %param.12) | copy-start | bytes 388
  0.7 1.8 %copy-start.7 = (s32[32,1]{0,1:T(1,128)S(1)}, s32[32,1]{0,1:T(1,128)}, u32[]{:S(2)}) copy-start(s32[32,1]{0,1:T(1,128)} %param.11) | copy-start | bytes 388
  0.7 1.8 %copy-start.3 = (bf16[32,50]{1,0:T(8,128)(2,1)S(1)}, bf16[32,50]{1,0:T(8,128)(2,1)}, u32[]{:S(2)}) copy-start(bf16[32,50]{1,0:T(8,128)(2,1)} %wave_ref.1) | copy-start | bytes 9604
  2.5 1.4 %copy-start = (bf16[1536,512]{1,0:T(8,128)(2,1)S(1)}, bf16[1536,512]{1,0:T(8,128)(2,1)}, u32[]{:S(2)}) copy-start(bf16[1536,512]{1,0:T(8,128)(2,1)} %w1_hbm.1) | copy-start | bytes 4718596
